TPU v7x, 32 devices: a whole 2x2x4 slice. The times are simulated.
32 devices in a mesh: snap: 4 (over y, x), space: 8 (over z, core).
Axes of the slice: x: 2, y: 2, z: 4, core: 2. Of those that a mesh axis runs over, the one named last changes fastest.
Arguments:
- field_in: bfloat16 [4, 8, 32, 32, 256], P('snap', 'space'), may hold values from -6 to 6
- ocean_mask: int32 [8, 32, 32], P('space'), may hold values 0 or 1
- cotangent: bfloat16 [4, 8, 32, 32, 256], P('snap', 'space'), may hold values from -6 to 6
- w_first: bfloat16 [3, 3, 256, 128], replicated, may hold values from -0.125 to 0.125
- b_first: float32 [128], replicated, may hold values from -3 to 3
- w_second: bfloat16 [3, 3, 128, 256], replicated, may hold values from -0.1875 to 0.1875
- b_second: float32 [256], replicated, may hold values from -3 to 3
Outputs:
- field_out: bfloat16 [4, 8, 32, 32, 256], P('snap', 'space')
- grad_field: bfloat16 [4, 8, 32, 32, 256], P('snap', 'space')
- grad_w_first: float32 [3, 3, 256, 128], P(None, None, 'space')
- grad_w_second: float32 [3, 3, 128, 256], P(None, None, 'space')
- grad_b_first: float32 [128], P('space')
- grad_b_second: float32 [256], P('space')
All inputs are finite; a program needn't handle non-finite values. No bound on the sum of `ocean_mask` on one device may be relied on, other than what follows from the above.
Results may differ from a plain program's by a relative error of at most 0.014.
Values may be sent and summed in bfloat16 or wider, within the bound.
A program may use at most 64 MiB of HBM per device.

v0:
```python
import math

import jax
import jax.numpy as jnp
from jax import lax
from jax.sharding import PartitionSpec as P

DEV_COLS = 4


ROOT_HALF = 0.7071067811865476
INV_ROOT_TWO_PI = 0.3989422804014327


def from_behind(array, axis, by):
    length = lax.axis_size(axis)
    return lax.ppermute(array, axis, [(i, (i + by) % length) for i in range(length)])


def gelu_value(pre):
    return 0.5 * pre * (1.0 + lax.erf(pre * ROOT_HALF))


def gelu_slope(pre):
    return (
        0.5 * (1.0 + lax.erf(pre * ROOT_HALF)) + pre * jnp.exp(-0.5 * pre * pre) * INV_ROOT_TWO_PI
    )


def dilated(padded, kernel):
    return lax.conv_general_dilated(
        padded[None],
        kernel,
        (1, 1),
        "VALID",
        rhs_dilation=(2, 2),
        dimension_numbers=("NHWC", "HWIO", "NHWC"),
        preferred_element_type=jnp.float32,
    )[0]


def flipped(kernel):
    return jnp.swapaxes(kernel[::-1, ::-1], 2, 3)


def tap_sums(padded, grad_out):
    span_y = grad_out.shape[0]
    span_x = grad_out.shape[1]
    flat_out = grad_out.reshape(span_y * span_x, grad_out.shape[2])
    tap_rows = []
    for tap_y in range(3):
        tap_line = []
        for tap_x in range(3):
            window = padded[2 * tap_y : 2 * tap_y + span_y, 2 * tap_x : 2 * tap_x + span_x].reshape(
                span_y * span_x, padded.shape[2]
            )
            tap_line.append(
                lax.dot_general(
                    window, flat_out, (((0,), (0,)), ((), ())), preferred_element_type=jnp.float32
                )
            )
        tap_rows.append(jnp.stack(tap_line))
    return jnp.stack(tap_rows)


def grid_halo(region):
    count = lax.axis_size("space")
    position = (lax.axis_index("space") + 1) % count
    column = position % DEV_COLS
    line = position // DEV_COLS
    last_line = count // DEV_COLS - 1
    strips = []
    for offset in (1, -1):
        edge_cells = region[:, -2:] if offset == 1 else region[:, :2]
        arrived = from_behind(edge_cells, "space", offset)
        inside = column != 0 if offset == 1 else column != DEV_COLS - 1
        strips.append(jnp.where(inside, arrived, jnp.zeros_like(arrived)))
    widened = jnp.concatenate([strips[0], region, strips[1]], axis=1)
    row_bands = []
    for offset in (DEV_COLS, -DEV_COLS):
        edge_cells = widened[-2:] if offset > 0 else widened[:2]
        arrived = from_behind(edge_cells, "space", offset)
        inside = line != 0 if offset > 0 else line != last_line
        row_bands.append(jnp.where(inside, arrived, jnp.zeros_like(arrived)))
    return jnp.concatenate([row_bands[0], widened, row_bands[1]], axis=0)


def local(field_in, ocean_mask, cotangent, w_first, b_first, w_second, b_second):
    region = field_in[0, 0]
    upstream = cotangent[0, 0]
    ocean = ocean_mask[0].astype(jnp.float32)[:, :, None]
    total = (
        field_in.shape[0]
        * lax.axis_size("snap")
        * lax.axis_size("space")
        * region.shape[0]
        * region.shape[1]
    )
    scale = 1.0 / math.sqrt(float(total))
    source_pad = grid_halo(region)
    pre = dilated(source_pad, w_first) + b_first
    hidden = (ocean * gelu_value(pre)).astype(jnp.bfloat16)
    hidden_pad = grid_halo(hidden)
    mixed = dilated(hidden_pad, w_second) + b_second
    field_out = (region.astype(jnp.float32) + ocean * mixed).astype(jnp.bfloat16)
    g_mixed = (ocean * upstream.astype(jnp.float32)).astype(jnp.bfloat16)
    grad_wb = tap_sums(hidden_pad, g_mixed)
    grad_bb = jnp.sum(g_mixed.astype(jnp.float32), axis=(0, 1))
    mixed_pad = grid_halo(g_mixed)
    g_hidden = dilated(mixed_pad, flipped(w_second))
    g_pre = (ocean * g_hidden * gelu_slope(pre)).astype(jnp.bfloat16)
    pre_pad = grid_halo(g_pre)
    g_input = (upstream.astype(jnp.float32) + dilated(pre_pad, flipped(w_first))).astype(
        jnp.bfloat16
    )
    grad_wa = tap_sums(source_pad, g_pre)
    grad_ba = jnp.sum(g_pre.astype(jnp.float32), axis=(0, 1))
    shares = (
        lax.psum_scatter(grad_wa, "space", scatter_dimension=2, tiled=True),
        lax.psum_scatter(grad_wb, "space", scatter_dimension=2, tiled=True),
        lax.psum_scatter(grad_ba, "space", scatter_dimension=0, tiled=True),
        lax.psum_scatter(grad_bb, "space", scatter_dimension=0, tiled=True),
    )
    summed = lax.psum((shares[0], shares[1], shares[2], shares[3]), "snap")
    return (
        field_out[None, None],
        g_input[None, None],
        summed[0] * scale,
        summed[1] * scale,
        summed[2] * scale,
        summed[3] * scale,
    )


def solution(mesh):
    placed = (
        P("snap", "space", None, None, None),
        P("space", None, None),
        P("snap", "space", None, None, None),
        P(),
        P(),
        P(),
        P(),
    )
    return jax.shard_map(
        local,
        mesh=mesh,
        in_specs=placed,
        out_specs=(
            P("snap", "space", None, None, None),
            P("snap", "space", None, None, None),
            P(None, None, "space", None),
            P(None, None, "space", None),
            P("space"),
            P("space"),
        ),
        check_vma=False,
    )
```

profile of v0, /device:TPU:0, one launch (start us, length us, event | category | flops | bytes accessed | tf_op | source)
XLA Modules:
  0.0 168.3 jit_solution(7899054096546081111)
XLA Ops:
  7.2 0.8 convert_bitcast_fusion.1
  8.1 1.3 convert_reduce_fusion
  9.4 0.5 collective-permute-start.8
  9.9 1.0 fusion.102
  10.9 2.7 %collective-permute-start = (bf16[32,2,256]{2,1,0:T(2,128)(2,1)S(1)}, bf16[32,2,256]{2,1,0:T(2,128)(2,1)S(1)}, u32[]{:S(2)}, u32[]{:S(2)}) collective-permute-start(bf16[32,2,256]{2,1,0:T(2,128)(2,1)S(1)} %get-tuple-element.29), channel_id=1, source_target_pairs={{0,1},{1,2},{2,3},{3,4},{4,5},{5,6},{6,7},{7,0},{8,9},{9,10},{10,1... | collective-permute-start | bytes 98312 | tf_op jit(solution)/shard_map/ppermute | solution.py:17
  13.6 1.4 collective-permute-start.1
  15.1 0.7 collective-permute-start.9
  15.9 1.5 collective-permute-done.9
  17.4 1.1 collective-permute-start.10
  18.7 1.9 %collective-permute-start.2 = (bf16[2,36,256]{2,1,0:T(8,128)(2,1)S(1)}, bf16[2,36,256]{2,1,0:T(8,128)(2,1)S(1)}, u32[]{:S(2)}, u32[]{:S(2)}) collective-permute-start(bf16[2,36,256]{2,1,0:T(8,128)(2,1)S(1)} %get-tuple-element.22), channel_id=1, source_target_pairs={{0,4},{1,5},{2,6},{3,7},{4,0},{5,1},{6,2},{7,3},{8,12},{9,13},{10,... | collective-permute-start | bytes 110600 | tf_op jit(solution)/shard_map/ppermute | solution.py:17
  20.6 1.0 collective-permute-start.3
  21.7 1.9 %collective-permute-start.11 = (bf16[2,36,256]{2,1,0:T(8,128)(2,1)S(1)}, bf16[2,36,256]{2,1,0:T(8,128)(2,1)S(1)}, u32[]{:S(2)}, u32[]{:S(2)}) collective-permute-start(bf16[2,36,256]{2,1,0:T(8,128)(2,1)S(1)} %get-tuple-element.21), channel_id=1, source_target_pairs={{0,4},{1,5},{2,6},{3,7},{4,0},{5,1},{6,2},{7,3},{8,12},{9,13},{10,... | collective-permute-start | bytes 110600 | tf_op jit(solution)/shard_map/ppermute | solution.py:17
  23.6 4.9 %collective-permute-done.11 = bf16[2,36,256]{2,1,0:T(8,128)(2,1)S(1)} collective-permute-done((bf16[2,36,256]{2,1,0:T(8,128)(2,1)S(1)}, bf16[2,36,256]{2,1,0:T(8,128)(2,1)S(1)}, u32[]{:S(2)}, u32[]{:S(2)}) %collective-permute-start.11) | collective-permute-done | bytes 36896 | tf_op jit(solution)/shard_map/ppermute | solution.py:17
  28.5 0.4 maximum_bitcast_fusion.1
  29.4 0.7 copy-done.5
  30.2 1.7 %fusion.18 = f32[32,8,5,128]{3,1,2,0:T(8,128)S(1)} fusion(bf16[3,3,128,256]{3,2,1,0:T(8,128)(2,1)S(1)} %copy-done.5, bf16[36,1,7,4,256]{4,2,3,0,1:T(8,128)(2,1)S(1)} %slice.164, bf16[36,1,8,5,256]{4,2,3,0,1:T(8,128)(2,1)S(1)} %copy.52, pred[8,5]{0,1:T(8,128)(4,1)S(1)} %copy-done.8), kind=kOutput, calls=%fused_computation.23 | convolution fusion | flops 759119872 | bytes 2498600 | tf_op jit(solution)/shard_map/conv_general_dilated | solution.py:31
  32.1 0.4 maximum_bitcast_fusion
  33.4 1.8 %multiply_multiply_fusion.2 = (f32[32,8,5,128]{3,1,2,0:T(8,128)S(1)}, f32[32,8,5,128]{3,1,2,0:T(8,128)S(1)}, f32[32,8,5,128]{3,1,2,0:T(8,128)S(1)}) fusion(f32[128]{0:T(128)S(1)} %copy-done.4, bf16[3,3,256,128]{3,2,1,0:T(8,128)(2,1)S(1)} %copy-done, bf16[36,1,7,4,256]{4,2,3,0,1:T(8,128)(2,1)S(1)} %slice.156, bf16[36,1,8,5,256]{4,2,3,0,1:T(8,128)(2,1)S(1)} %copy.42, ...), kind=kOutput, calls=%fused_computation.79 | convolution fusion | flops 760922112 | bytes 3809832 | tf_op jit(solution)/shard_map/conv_general_dilated | solution.py:31
  35.4 0.8 convert_reduce_fusion.1
  36.2 0.4 convolution_bitcast_fusion.12
  36.6 0.3 convolution_bitcast_fusion.14
  37.0 0.4 maximum_maximum_fusion
  38.0 0.3 convolution_bitcast_fusion.17
  39.7 0.6 fusion.67
  40.5 3.5 %collective-permute-start.5 = (bf16[32,2,128]{2,1,0:T(2,128)(2,1)S(1)}, bf16[32,2,128]{2,1,0:T(2,128)(2,1)S(1)}, u32[]{:S(2)}, u32[]{:S(2)}) collective-permute-start(bf16[32,2,128]{2,1,0:T(2,128)(2,1)S(1)} %get-tuple-element.40), channel_id=1, source_target_pairs={{0,7},{1,0},{2,1},{3,2},{4,3},{5,4},{6,5},{7,6},{8,15},{9,8},{10,9... | collective-permute-start | bytes 49160 | tf_op jit(solution)/shard_map/ppermute | solution.py:17
  44.0 3.5 %collective-permute-start.13 = (bf16[32,2,128]{2,1,0:T(2,128)(2,1)S(1)}, bf16[32,2,128]{2,1,0:T(2,128)(2,1)S(1)}, u32[]{:S(2)}, u32[]{:S(2)}) collective-permute-start(bf16[32,2,128]{2,1,0:T(2,128)(2,1)S(1)} %get-tuple-element.38), channel_id=1, source_target_pairs={{0,7},{1,0},{2,1},{3,2},{4,3},{5,4},{6,5},{7,6},{8,15},{9,8},{10,9... | collective-permute-start | bytes 49160 | tf_op jit(solution)/shard_map/ppermute | solution.py:17
  47.5 0.3 convolution_bitcast_fusion.13
  48.0 1.1 pad_maximum_fusion
  50.2 3.0 %collective-permute-start.14 = (bf16[2,36,128]{2,1,0:T(8,128)(2,1)S(1)}, bf16[2,36,128]{2,1,0:T(8,128)(2,1)S(1)}, u32[]{:S(2)}, u32[]{:S(2)}) collective-permute-start(bf16[2,36,128]{2,1,0:T(8,128)(2,1)S(1)} %get-tuple-element.33), channel_id=1, source_target_pairs={{0,4},{1,5},{2,6},{3,7},{4,0},{5,1},{6,2},{7,3},{8,12},{9,13},{10,... | collective-permute-start | bytes 55304 | tf_op jit(solution)/shard_map/ppermute | solution.py:17
  53.2 2.8 %collective-permute-start.7 = (bf16[2,36,128]{2,1,0:T(8,128)(2,1)S(1)}, bf16[2,36,128]{2,1,0:T(8,128)(2,1)S(1)}, u32[]{:S(2)}, u32[]{:S(2)}) collective-permute-start(bf16[2,36,128]{2,1,0:T(8,128)(2,1)S(1)} %get-tuple-element.36), channel_id=1, source_target_pairs={{0,4},{1,5},{2,6},{3,7},{4,0},{5,1},{6,2},{7,3},{8,12},{9,13},{10,... | collective-permute-start | bytes 55304 | tf_op jit(solution)/shard_map/ppermute | solution.py:17
  56.1 2.8 %collective-permute-done.7 = bf16[2,36,128]{2,1,0:T(8,128)(2,1)S(1)} collective-permute-done((bf16[2,36,128]{2,1,0:T(8,128)(2,1)S(1)}, bf16[2,36,128]{2,1,0:T(8,128)(2,1)S(1)}, u32[]{:S(2)}, u32[]{:S(2)}) %collective-permute-start.7) | collective-permute-done | bytes 18464 | tf_op jit(solution)/shard_map/ppermute | solution.py:17
  60.0 0.8 copy-done.6
  60.8 1.0 convolution_select_fusion.1
  61.8 0.4 copy.48
  62.4 1.1 convolution_select_fusion
  63.5 0.4 copy.58
  65.9 2.2 %fusion.56 = (bf16[32,32,256]{2,1,0:T(8,128)(2,1)S(1)}, bf16[1,1,32,32,256]{4,3,2,1,0:T(8,128)(2,1)}, bf16[1,1,32,32,256]{4,3,2,1,0:T(8,128)(2,1)}) fusion(bf16[1,1,32,32,256]{4,3,2,1,0:T(8,128)(2,1)S(1)} %copy-done.2, f32[32,32]{1,0:T(8,128)S(1)} %convert_bitcast_fusion.1, f32[32,1,32,256]{3,0,2,1:T(8,128)S(1)} %slice.169, f32[256]{0:T(256)S(1)} %copy-done.3, ...), kind=kLoop, calls=%fused_computation.86 | loop fusion | flops 2621440 | bytes 4723712 | tf_op jit(solution)/shard_map/convert_element_type | solution.py:106
  68.2 0.6 convolution_bitcast_fusion.4
  68.8 1.1 pad_maximum_fusion.1
  70.1 0.6 dynamic-slice
  71.9 13.9 %all-reduce.2 = (f32[128]{0:T(128)S(1)}, f32[256]{0:T(256)S(1)}) all-reduce(f32[128]{0:T(128)S(1)} %get-tuple-element.14, f32[256]{0:T(256)S(1)} %get-tuple-element.12), channel_id=4, replica_groups=mesh['snap'=4,'space'=8] {'space'}, use_global_device_ids=true, to_apply=%region_5.6.clone | all-reduce | flops 384 | bytes 3072
  86.0 10.0 %all-reduce.3 = (f32[16]{0:T(128)S(1)}, f32[32]{0:T(128)S(1)}) all-reduce(f32[16]{0:T(128)S(1)} %dynamic-slice.1, f32[32]{0:T(128)S(1)} %dynamic-slice.3), channel_id=1, replica_groups=mesh['snap'=4,'space'=8] {'snap'}, use_global_device_ids=true, to_apply=%region_6.7 | all-reduce | flops 48 | bytes 384 | tf_op jit(solution)/shard_map/psum | solution.py:124
  96.0 17.9 %reduce-scatter.5.cloned.1.call-done = f32[3,3,16,256]{3,2,1,0:T(8,128)} async-done(((f32[3,3,128,256]{3,2,1,0:T(8,128)}), f32[3,3,16,256]{3,2,1,0:T(8,128)}) %reduce-scatter.5.cloned.1.call-update) | async-done | bytes 147472 | tf_op jit(solution)/shard_map/reduce_scatter | solution.py:120
  113.9 0.5 broadcast_multiply_fusion.3
  114.5 0.5 broadcast_multiply_fusion.2
  115.0 43.6 %all-reduce.7.cloned.1.call-done = (f32[3,3,32,128]{3,2,1,0:T(8,128)}, f32[3,3,16,256]{3,2,1,0:T(8,128)}) async-done(((f32[3,3,32,128]{3,2,1,0:T(8,128)}, f32[3,3,16,256]{3,2,1,0:T(8,128)}), (f32[3,3,32,128]{3,2,1,0:T(8,128)}, f32[3,3,16,256]{3,2,1,0:T(8,128)})) %all-reduce.7.cloned.1.call-update) | async-done | bytes 294928 | tf_op jit(solution)/shard_map/psum | solution.py:124
  158.6 1.6 broadcast_multiply_fusion.1
  160.2 1.6 broadcast_multiply_fusion
  (111 shorter events, 8.7 us)
Async XLA Ops:
  7.2 25.9 %copy-start = (bf16[3,3,256,128]{3,2,1,0:T(8,128)(2,1)S(1)}, bf16[3,3,256,128]{3,2,1,0:T(8,128)(2,1)}, u32[]{:S(2)}) copy-start(bf16[3,3,256,128]{3,2,1,0:T(8,128)(2,1)} %param.10) | copy-start | bytes 1769476
  7.2 11.4 %copy-start.1 = (bf16[1,1,32,32,256]{4,3,2,1,0:T(8,128)(2,1)S(1)}, bf16[1,1,32,32,256]{4,3,2,1,0:T(8,128)(2,1)}, u32[]{:S(2)}) copy-start(bf16[1,1,32,32,256]{4,3,2,1,0:T(8,128)(2,1)} %param.7) | copy-start | bytes 1572868
  7.2 88.8 %reduce-scatter.3.cloned.1.call-start = ((), (), s32[]{:S(2)}) async-start(), calls=%async_computation.2 | async-start | bytes 1327104 | tf_op jit(solution)/shard_map/reduce_scatter | solution.py:119
  9.4 6.5 %collective-permute-start.8 = (bf16[32,2,256]{2,1,0:T(2,128)(2,1)S(1)}, bf16[32,2,256]{2,1,0:T(2,128)(2,1)S(1)}, u32[]{:S(2)}, u32[]{:S(2)}) collective-permute-start(bf16[32,2,256]{2,1,0:T(2,128)(2,1)S(1)} %get-tuple-element.27), channel_id=1, source_target_pairs={{0,1},{1,2},{2,3},{3,4},{4,5},{5,6},{6,7},{7,0},{8,9},{9,10},{10,1... | collective-permute-start | bytes 98312 | tf_op jit(solution)/shard_map/ppermute | solution.py:17
  10.9 7.6 %collective-permute-start = (bf16[32,2,256]{2,1,0:T(2,128)(2,1)S(1)}, bf16[32,2,256]{2,1,0:T(2,128)(2,1)S(1)}, u32[]{:S(2)}, u32[]{:S(2)}) collective-permute-start(bf16[32,2,256]{2,1,0:T(2,128)(2,1)S(1)} %get-tuple-element.29), channel_id=1, source_target_pairs={{0,1},{1,2},{2,3},{3,4},{4,5},{5,6},{6,7},{7,0},{8,9},{9,10},{10,1... | collective-permute-start | bytes 98312 | tf_op jit(solution)/shard_map/ppermute | solution.py:17
  13.6 4.9 %collective-permute-start.1 = (bf16[32,2,256]{2,1,0:T(2,128)(2,1)S(1)}, bf16[32,2,256]{2,1,0:T(2,128)(2,1)S(1)}, u32[]{:S(2)}, u32[]{:S(2)}) collective-permute-start(bf16[32,2,256]{2,1,0:T(2,128)(2,1)S(1)} %get-tuple-element.30), channel_id=1, source_target_pairs={{0,7},{1,0},{2,1},{3,2},{4,3},{5,4},{6,5},{7,6},{8,15},{9,8},{10,9... | collective-permute-start | bytes 98312 | tf_op jit(solution)/shard_map/ppermute | solution.py:17
  15.1 2.3 %collective-permute-start.9 = (bf16[32,2,256]{2,1,0:T(2,128)(2,1)S(1)}, bf16[32,2,256]{2,1,0:T(2,128)(2,1)S(1)}, u32[]{:S(2)}, u32[]{:S(2)}) collective-permute-start(bf16[32,2,256]{2,1,0:T(2,128)(2,1)S(1)} %get-tuple-element.28), channel_id=1, source_target_pairs={{0,7},{1,0},{2,1},{3,2},{4,3},{5,4},{6,5},{7,6},{8,15},{9,8},{10,9... | collective-permute-start | bytes 98312 | tf_op jit(solution)/shard_map/ppermute | solution.py:17
  17.4 6.1 %collective-permute-start.10 = (bf16[2,36,256]{2,1,0:T(8,128)(2,1)S(1)}, bf16[2,36,256]{2,1,0:T(8,128)(2,1)S(1)}, u32[]{:S(2)}, u32[]{:S(2)}) collective-permute-start(bf16[2,36,256]{2,1,0:T(8,128)(2,1)S(1)} %get-tuple-element.20), channel_id=1, source_target_pairs={{0,4},{1,5},{2,6},{3,7},{4,0},{5,1},{6,2},{7,3},{8,12},{9,13},{10,... | collective-permute-start | bytes 110600 | tf_op jit(solution)/shard_map/ppermute | solution.py:17
  18.7 13.2 %collective-permute-start.2 = (bf16[2,36,256]{2,1,0:T(8,128)(2,1)S(1)}, bf16[2,36,256]{2,1,0:T(8,128)(2,1)S(1)}, u32[]{:S(2)}, u32[]{:S(2)}) collective-permute-start(bf16[2,36,256]{2,1,0:T(8,128)(2,1)S(1)} %get-tuple-element.22), channel_id=1, source_target_pairs={{0,4},{1,5},{2,6},{3,7},{4,0},{5,1},{6,2},{7,3},{8,12},{9,13},{10,... | collective-permute-start | bytes 110600 | tf_op jit(solution)/shard_map/ppermute | solution.py:17
  20.6 11.5 %collective-permute-start.3 = (bf16[2,36,256]{2,1,0:T(8,128)(2,1)S(1)}, bf16[2,36,256]{2,1,0:T(8,128)(2,1)S(1)}, u32[]{:S(2)}, u32[]{:S(2)}) collective-permute-start(bf16[2,36,256]{2,1,0:T(8,128)(2,1)S(1)} %get-tuple-element.23), channel_id=1, source_target_pairs={{0,4},{1,5},{2,6},{3,7},{4,0},{5,1},{6,2},{7,3},{8,12},{9,13},{10,... | collective-permute-start | bytes 110600 | tf_op jit(solution)/shard_map/ppermute | solution.py:17
  21.7 6.8 %collective-permute-start.11 = (bf16[2,36,256]{2,1,0:T(8,128)(2,1)S(1)}, bf16[2,36,256]{2,1,0:T(8,128)(2,1)S(1)}, u32[]{:S(2)}, u32[]{:S(2)}) collective-permute-start(bf16[2,36,256]{2,1,0:T(8,128)(2,1)S(1)} %get-tuple-element.21), channel_id=1, source_target_pairs={{0,4},{1,5},{2,6},{3,7},{4,0},{5,1},{6,2},{7,3},{8,12},{9,13},{10,... | collective-permute-start | bytes 110600 | tf_op jit(solution)/shard_map/ppermute | solution.py:17
  29.1 1.1 copy-start.5
  29.1 1.1 copy-start.8
  32.8 0.7 copy-start.4
  40.4 9.3 %collective-permute-start.4 = (bf16[32,2,128]{2,1,0:T(2,128)(2,1)S(1)}, bf16[32,2,128]{2,1,0:T(2,128)(2,1)S(1)}, u32[]{:S(2)}, u32[]{:S(2)}) collective-permute-start(bf16[32,2,128]{2,1,0:T(2,128)(2,1)S(1)} %get-tuple-element.39), channel_id=1, source_target_pairs={{0,1},{1,2},{2,3},{3,4},{4,5},{5,6},{6,7},{7,0},{8,9},{9,10},{10,1... | collective-permute-start | bytes 49160 | tf_op jit(solution)/shard_map/ppermute | solution.py:17
  40.5 8.9 %collective-permute-start.5 = (bf16[32,2,128]{2,1,0:T(2,128)(2,1)S(1)}, bf16[32,2,128]{2,1,0:T(2,128)(2,1)S(1)}, u32[]{:S(2)}, u32[]{:S(2)}) collective-permute-start(bf16[32,2,128]{2,1,0:T(2,128)(2,1)S(1)} %get-tuple-element.40), channel_id=1, source_target_pairs={{0,7},{1,0},{2,1},{3,2},{4,3},{5,4},{6,5},{7,6},{8,15},{9,8},{10,9... | collective-permute-start | bytes 49160 | tf_op jit(solution)/shard_map/ppermute | solution.py:17
  44.0 6.1 %collective-permute-start.12 = (bf16[32,2,128]{2,1,0:T(2,128)(2,1)S(1)}, bf16[32,2,128]{2,1,0:T(2,128)(2,1)S(1)}, u32[]{:S(2)}, u32[]{:S(2)}) collective-permute-start(bf16[32,2,128]{2,1,0:T(2,128)(2,1)S(1)} %get-tuple-element.37), channel_id=1, source_target_pairs={{0,1},{1,2},{2,3},{3,4},{4,5},{5,6},{6,7},{7,0},{8,9},{9,10},{10,1... | collective-permute-start | bytes 49160 | tf_op jit(solution)/shard_map/ppermute | solution.py:17
  44.0 6.1 %collective-permute-start.13 = (bf16[32,2,128]{2,1,0:T(2,128)(2,1)S(1)}, bf16[32,2,128]{2,1,0:T(2,128)(2,1)S(1)}, u32[]{:S(2)}, u32[]{:S(2)}) collective-permute-start(bf16[32,2,128]{2,1,0:T(2,128)(2,1)S(1)} %get-tuple-element.38), channel_id=1, source_target_pairs={{0,7},{1,0},{2,1},{3,2},{4,3},{5,4},{6,5},{7,6},{8,15},{9,8},{10,9... | collective-permute-start | bytes 49160 | tf_op jit(solution)/shard_map/ppermute | solution.py:17
  49.1 64.8 %reduce-scatter.5.cloned.1.call-start = ((), (), s32[]{:S(2)}) async-start(), calls=%async_computation.3 | async-start | bytes 1327104 | tf_op jit(solution)/shard_map/reduce_scatter | solution.py:120
  50.0 6.1 %collective-permute-start.6 = (bf16[2,36,128]{2,1,0:T(8,128)(2,1)S(1)}, bf16[2,36,128]{2,1,0:T(8,128)(2,1)S(1)}, u32[]{:S(2)}, u32[]{:S(2)}) collective-permute-start(bf16[2,36,128]{2,1,0:T(8,128)(2,1)S(1)} %get-tuple-element.35), channel_id=1, source_target_pairs={{0,4},{1,5},{2,6},{3,7},{4,0},{5,1},{6,2},{7,3},{8,12},{9,13},{10,... | collective-permute-start | bytes 55304 | tf_op jit(solution)/shard_map/ppermute | solution.py:17
  50.2 8.9 %collective-permute-start.14 = (bf16[2,36,128]{2,1,0:T(8,128)(2,1)S(1)}, bf16[2,36,128]{2,1,0:T(8,128)(2,1)S(1)}, u32[]{:S(2)}, u32[]{:S(2)}) collective-permute-start(bf16[2,36,128]{2,1,0:T(8,128)(2,1)S(1)} %get-tuple-element.33), channel_id=1, source_target_pairs={{0,4},{1,5},{2,6},{3,7},{4,0},{5,1},{6,2},{7,3},{8,12},{9,13},{10,... | collective-permute-start | bytes 55304 | tf_op jit(solution)/shard_map/ppermute | solution.py:17
  53.2 6.1 %collective-permute-start.15 = (bf16[2,36,128]{2,1,0:T(8,128)(2,1)S(1)}, bf16[2,36,128]{2,1,0:T(8,128)(2,1)S(1)}, u32[]{:S(2)}, u32[]{:S(2)}) collective-permute-start(bf16[2,36,128]{2,1,0:T(8,128)(2,1)S(1)} %get-tuple-element.34), channel_id=1, source_target_pairs={{0,4},{1,5},{2,6},{3,7},{4,0},{5,1},{6,2},{7,3},{8,12},{9,13},{10,... | collective-permute-start | bytes 55304 | tf_op jit(solution)/shard_map/ppermute | solution.py:17
  53.2 5.6 %collective-permute-start.7 = (bf16[2,36,128]{2,1,0:T(8,128)(2,1)S(1)}, bf16[2,36,128]{2,1,0:T(8,128)(2,1)S(1)}, u32[]{:S(2)}, u32[]{:S(2)}) collective-permute-start(bf16[2,36,128]{2,1,0:T(8,128)(2,1)S(1)} %get-tuple-element.36), channel_id=1, source_target_pairs={{0,4},{1,5},{2,6},{3,7},{4,0},{5,1},{6,2},{7,3},{8,12},{9,13},{10,... | collective-permute-start | bytes 55304 | tf_op jit(solution)/shard_map/ppermute | solution.py:17
  59.7 1.1 copy-start.6
  64.9 1.0 copy-start.2
  64.9 1.0 copy-start.3
  68.8 1.2 copy-start.7
  70.0 88.6 %all-reduce.7.cloned.1.call-start = ((), (), s32[]{:S(2)}) async-start(), calls=%async_computation.4 | async-start | bytes 589824 | tf_op jit(solution)/shard_map/psum | solution.py:124
Sparse Core Ops, SparseCore 0:
  49.2 31.0 reduce-scatter.2
  82.6 31.2 reduce-scatter.4
  116.9 41.6 all-reduce.6
where the time goes:
time: 169 us; the launch traced here: 168 us
  waiting for transfers between devices  70.8 us (42%)
  starting transfers between devices  24.7 us (15%)
  blocking collectives  23.9 us (14%)
  between operations  15.8 us (9%)
  other arithmetic  14.5 us (9%)
  matrix products  11.4 us (7%)
  local copies, waits for them, and re-layouts  7.18 us (4%)
    psum x1, waiting for transfers between devices, local(): summed = lax.psum((shares[0], shares[1], shares[2], shares[3]), 'snap')  43.6 us
    ppermute x16, starting transfers between devices, from_behind(): lax.ppermute(array, axis, [(i, (i + by) % length) for i in range(length)])  24.4 us
    reduce_scatter x1, waiting for transfers between devices, local(): lax.psum_scatter(grad_wb, 'space', scatter_dimension=2, tiled=True)  17.9 us
    unnamed x1, blocking collectives  13.9 us
    psum x1, blocking collectives, local(): summed = lax.psum((shares[0], shares[1], shares[2], shares[3]), 'snap')  10 us
    ppermute x16, waiting for transfers between devices, from_behind(): lax.ppermute(array, axis, [(i, (i + by) % length) for i in range(length)])  9.21 us
    dot_general x18, matrix products, tap_sums(): lax.dot_general(window, flat_out, (((0,), (0,)), ((), ())), preferred_ele...  5.82 us
    conv_general_dilated x4, matrix products, dilated(): lax.conv_general_dilated(padded[None], kernel, (1, 1), 'VALID', rhs_dilat...  5.6 us
  transfers between devices with their start and end apart: 19, of which 5 were waited for; matrix products, arithmetic and copies ran while one was open for 11% of the time, Pallas kernels for 0%

commit v1 on v0

v1 whole, which is shorter than its diff:
```python
import functools
import math

import jax
import jax.numpy as jnp
from jax import lax
from jax.experimental import pallas as pl
from jax.experimental.pallas import tpu as pltpu
from jax.sharding import PartitionSpec as P

DEV_COLS = 4
ROOT_HALF = 0.7071067811865476
INV_ROOT_TWO_PI = 0.3989422804014327
MESH = pl.DeviceIdType.MESH
F32 = jnp.float32
BF16 = jnp.bfloat16

DIRS = ((-1, 0), (1, 0), (0, -1), (0, 1), (-1, -1), (-1, 1), (1, -1), (1, 1))
UP, DOWN, LEFT, RIGHT, UP_LEFT, UP_RIGHT, DOWN_LEFT, DOWN_RIGHT = range(8)
OPPOSITE = (DOWN, UP, RIGHT, LEFT, DOWN_RIGHT, DOWN_LEFT, UP_RIGHT, UP_LEFT)

WIDE = 32
TALL = 32
CELLS = TALL * WIDE
BAND = 2 * WIDE
BLOCK = 8 * WIDE
BLOCKS = CELLS // BLOCK
EDGE = 2 * TALL
PART = 16


def mm(a, b, dims=(((1,), (0,)), ((), ()))):
    return lax.dot_general(a, b, dims, preferred_element_type=F32)


NT = (((1,), (1,)), ((), ()))
TN = (((0,), (0,)), ((), ()))


def grid2(rows, columns):
    return (
        lax.broadcasted_iota(jnp.int32, (rows, columns), 0),
        lax.broadcasted_iota(jnp.int32, (rows, columns), 1),
    )


def onehot(condition):
    return jnp.where(condition, 1.0, 0.0).astype(BF16)


def shift_left_source(rows):
    r, c = grid2(rows, rows)
    return onehot((c == r - 2) & ((r & (WIDE - 1)) >= 2))


def shift_right_source(rows):
    r, c = grid2(rows, rows)
    return onehot((c == r + 2) & ((r & (WIDE - 1)) < WIDE - 2))


def left_insert(rows, first):
    r, h = grid2(rows, PART)
    x = r & (WIDE - 1)
    return onehot((x < 2) & (h == first + 2 * (r >> 5) + x))


def right_insert(rows, first):
    r, h = grid2(rows, PART)
    x = r & (WIDE - 1)
    return onehot((x >= WIDE - 2) & (h == first + 2 * (r >> 5) + x - (WIDE - 2)))


def left_pack():
    h, r = grid2(PART, BLOCK)
    x = r & (WIDE - 1)
    return onehot((x < 2) & (h == 2 * (r >> 5) + x))


def right_pack():
    h, r = grid2(PART, BLOCK)
    x = r & (WIDE - 1)
    return onehot((x >= WIDE - 2) & (h == 2 * (r >> 5) + x - (WIDE - 2)))


def rows_of(index, size, offset=0):
    return pl.ds(pl.multiple_of(index * size + offset, 16), size)


class Halo:
    def __init__(self, geometry, own, packs, bands, corners, send_sem, recv_sem):
        self.exists, self.peer = geometry
        self.own, self.packs, self.bands, self.corners = own, packs, bands, corners
        sources = (
            own.at[pl.ds(0, BAND)],
            own.at[pl.ds(CELLS - BAND, BAND)],
            packs.at[0],
            packs.at[1],
            packs.at[0, pl.ds(0, PART)],
            packs.at[1, pl.ds(0, PART)],
            packs.at[0, pl.ds(EDGE - PART, PART)],
            packs.at[1, pl.ds(EDGE - PART, PART)],
        )
        self.copies = []
        for d in range(8):
            slot = OPPOSITE[d]
            self.copies.append(
                pltpu.make_async_remote_copy(
                    src_ref=sources[d],
                    dst_ref=self.slot(slot),
                    send_sem=send_sem.at[d],
                    recv_sem=recv_sem.at[slot],
                    device_id={"space": self.peer[d]},
                    device_id_type=MESH,
                )
            )

    def slot(self, slot):
        return self.bands.at[slot] if slot < 4 else self.corners.at[slot - 4]

    def clear_missing(self):
        for d in range(8):
            ref = self.slot(d)

            @pl.when(jnp.logical_not(self.exists[d]))
            def _():
                ref[...] = jnp.zeros(ref.shape, ref.dtype)

    def pack(self):
        to_left, to_right = left_pack(), right_pack()
        for i in range(BLOCKS):
            cells = self.own[pl.ds(i * BLOCK, BLOCK), :]
            self.packs[0, pl.ds(i * PART, PART), :] = mm(to_left, cells).astype(BF16)
            self.packs[1, pl.ds(i * PART, PART), :] = mm(to_right, cells).astype(BF16)

    def start(self):
        for d in range(8):

            @pl.when(self.exists[d])
            def _():
                self.copies[d].start()

    def wait_recv(self):
        for d in range(8):

            @pl.when(self.exists[OPPOSITE[d]])
            def _():
                self.copies[d].wait_recv()

    def wait_send(self):
        for d in range(8):

            @pl.when(self.exists[d])
            def _():
                self.copies[d].wait_send()

    def interior(self, outs, width):
        from_left, from_right = shift_left_source(BLOCK), shift_right_source(BLOCK)

        def body(i, carry):
            cells = self.own[rows_of(i, BLOCK), :]
            there = rows_of(i, BLOCK, BAND)
            shifted = (
                mm(from_left, cells).astype(BF16),
                cells,
                mm(from_right, cells).astype(BF16),
            )
            for b in range(3):
                for n, out in enumerate(outs):
                    out[there, pl.ds(b * width, width)] = shifted[b][
                        :, n * width : (n + 1) * width
                    ]
            return carry

        lax.fori_loop(0, BLOCKS, body, 0)

    def borders(self, outs, width):
        into_left, into_right = left_insert(BLOCK, 0), right_insert(BLOCK, 0)

        def body(i, carry):
            there = rows_of(i, BLOCK, BAND)
            left = mm(into_left, self.bands[LEFT, rows_of(i, PART), :]).astype(BF16)
            right = mm(into_right, self.bands[RIGHT, rows_of(i, PART), :]).astype(BF16)
            for n, out in enumerate(outs):
                mine = slice(n * width, (n + 1) * width)
                out[there, pl.ds(0, width)] = out[there, pl.ds(0, width)] + left[:, mine]
                out[there, pl.ds(2 * width, width)] = (
                    out[there, pl.ds(2 * width, width)] + right[:, mine]
                )
            return carry

        lax.fori_loop(0, BLOCKS, body, 0)
        from_left, from_right = shift_left_source(BAND), shift_right_source(BAND)
        for band, first, where, side in (
            (UP, PART - 4, 0, (UP_LEFT, UP_RIGHT)),
            (DOWN, 0, CELLS + BAND, (DOWN_LEFT, DOWN_RIGHT)),
        ):
            cells = self.bands[band]
            shifted = (
                (
                    mm(from_left, cells)
                    + mm(left_insert(BAND, first), self.corners[side[0] - 4])
                ).astype(BF16),
                cells,
                (
                    mm(from_right, cells)
                    + mm(right_insert(BAND, first), self.corners[side[1] - 4])
                ).astype(BF16),
            )
            for b in range(3):
                for n, out in enumerate(outs):
                    out[pl.ds(where, BAND), pl.ds(b * width, width)] = shifted[b][
                        :, n * width : (n + 1) * width
                    ]


class Reduction:
    def __init__(self, n_space, n_snap, share, a_in, q, b_in, t, c_in, u, d_in, sems):
        self.n_chip, self.n_snap = n_space // 2, n_snap
        self.share, self.a_in, self.q, self.b_in = share, a_in, q, b_in
        self.t, self.c_in, self.u, self.d_in = t, c_in, u, d_in
        me = lax.axis_index("space")
        snap = lax.axis_index("snap")
        self.core = lax.rem(me, 2)
        self.chip = lax.div(me, 2)
        self.snap = snap
        a_s, a_r, b_s, b_r, c_s, c_r, d_s, d_r = sems

        def copy(src, dst, send, recv, device):
            return pltpu.make_async_remote_copy(
                src_ref=src,
                dst_ref=dst,
                send_sem=send,
                recv_sem=recv,
                device_id=device,
                device_id_type=MESH,
            )

        self.a = [copy(share.at[1 - self.core], a_in, a_s, a_r, {"space": me + 1 - 2 * self.core})]
        self.b, self.c, self.d = [], [], []
        for j in range(1, n_snap):
            other = lax.rem(snap + j, n_snap)
            self.b.append(
                copy(q.at[other], b_in.at[j - 1], b_s.at[j - 1], b_r.at[j - 1], {"snap": other})
            )
            self.d.append(
                copy(u, d_in.at[j - 1], d_s.at[j - 1], d_r.at[j - 1], {"snap": other})
            )
        for j in range(1, self.n_chip):
            other = lax.rem(self.chip + j, self.n_chip)
            self.c.append(
                copy(
                    t.at[other],
                    c_in.at[j - 1],
                    c_s.at[j - 1],
                    c_r.at[j - 1],
                    {"space": 2 * other + self.core},
                )
            )

    def start_a(self):
        self.a[0].start()

    def start_b(self):
        self.a[0].wait_recv()
        for z in range(self.n_chip):
            for k in range(self.n_snap):
                both = self.share[self.core, z, k].astype(F32) + self.a_in[z, k].astype(F32)
                self.q[k, z] = both.astype(BF16)
        for c in self.b:
            c.start()

    def start_c(self):
        for c in self.b:
            c.wait_recv()
        for z in range(self.n_chip):
            total = self.q[self.snap, z].astype(F32)
            for j in range(self.n_snap - 1):
                total += self.b_in[j, z].astype(F32)
            self.t[z] = total.astype(BF16)
        for c in self.c:
            c.start()

    def start_d(self):
        for c in self.c:
            c.wait_recv()
        total = self.t[self.chip].astype(F32)
        for j in range(self.n_chip - 1):
            total += self.c_in[j].astype(F32)
        self.u[...] = total.astype(BF16)
        for c in self.d:
            c.start()

    def finish(self, scale, whole):
        for c in self.d:
            c.wait_recv()
        whole[self.snap] = self.u[...].astype(F32) * scale
        for j in range(1, self.n_snap):
            sender = lax.rem(self.snap + self.n_snap - j, self.n_snap)
            whole[sender] = self.d_in[j - 1].astype(F32) * scale

    def wait_send(self):
        for c in self.a + self.b + self.c + self.d:
            c.wait_send()


def kernel(n_space, n_snap, fused, scale, *refs):
    refs = list(refs)

    def take(count):
        got = refs[:count]
        del refs[:count]
        return got

    field, mask, cot, w1, b1, w2, b2 = take(7)
    field_out, grad_field, gw1, gw2, gb1, gb2 = take(6)
    fg, fg_packs, fg_bands, fg_corners, f3, g3, fg_send, fg_recv = take(8)
    hp, hp_packs, hp_bands, hp_corners, h3, p3, hp_send, hp_recv = take(8)
    mfull, hall, pall = take(3)
    channels, hidden_channels = field.shape[1], hp.shape[1] // 2

    me = lax.axis_index("space")
    position = lax.rem(me + 1, n_space)
    line, column = lax.div(position, DEV_COLS), lax.rem(position, DEV_COLS)
    lines = n_space // DEV_COLS
    exists, peer = [], []
    for dy, dx in DIRS:
        there = None
        if dy:
            there = (line > 0) if dy < 0 else (line < lines - 1)
        if dx:
            inside = (column > 0) if dx < 0 else (column < DEV_COLS - 1)
            there = inside if there is None else jnp.logical_and(there, inside)
        exists.append(there)
        peer.append(lax.rem(position + DEV_COLS * dy + dx - 1 + 2 * n_space, n_space))
    geometry = (exists, peer)

    reductions = []
    if fused:
        for _ in range(2):
            share, a_in, q, b_in, t, c_in, u, d_in = take(8)
            sems = take(8)
            reductions.append(
                Reduction(n_space, n_snap, share, a_in, q, b_in, t, c_in, u, d_in, sems)
            )
        (whole,) = take(1)

    first = Halo(geometry, fg, fg_packs, fg_bands, fg_corners, fg_send, fg_recv)
    second = Halo(geometry, hp, hp_packs, hp_bands, hp_corners, hp_send, hp_recv)
    first.clear_missing()
    second.clear_missing()

    barrier = pltpu.get_barrier_semaphore()
    expected = jnp.int32(0)
    for d in range(8):

        @pl.when(exists[d])
        def _():
            pl.semaphore_signal(barrier, inc=1, device_id={"space": peer[d]}, device_id_type=MESH)

        expected = expected + exists[d].astype(jnp.int32)
    if fused:
        core = lax.rem(me, 2)
        pl.semaphore_signal(
            barrier, inc=1, device_id={"space": me + 1 - 2 * core}, device_id_type=MESH
        )
        for j in range(1, n_snap):
            other = lax.rem(lax.axis_index("snap") + j, n_snap)
            pl.semaphore_signal(barrier, inc=1, device_id={"snap": other}, device_id_type=MESH)
        for j in range(1, n_space // 2):
            other = lax.rem(lax.div(me, 2) + j, n_space // 2)
            pl.semaphore_signal(
                barrier, inc=1, device_id={"space": 2 * other + core}, device_id_type=MESH
            )
        expected = expected + (1 + n_snap - 1 + n_space // 2 - 1)

    mask_bits = mask[...].astype(F32).astype(BF16)

    def prepare(i, carry):
        here = rows_of(i, BLOCK)
        r, y = grid2(BLOCK, TALL)
        lines_of = mm(onehot((r >> 5) + i * (BLOCK // WIDE) == y), mask_bits)
        r, x = grid2(BLOCK, WIDE)
        one = jnp.where((r & (WIDE - 1)) == x, lines_of, 0.0).astype(BF16)
        m = mm(one, jnp.ones((WIDE, 128), BF16))
        mfull[here, :] = m
        fg[here, pl.ds(0, channels)] = field[here, :]
        for half in range(channels // 128):
            lanes = pl.ds(half * 128, 128)
            fg[here, pl.ds(channels + half * 128, 128)] = (
                cot[here, lanes].astype(F32) * m
            ).astype(BF16)
        return carry

    lax.fori_loop(0, BLOCKS, prepare, 0)
    first.pack()
    pl.semaphore_wait(barrier, expected)
    first.start()
    first.interior((f3, g3), channels)
    pad = jnp.zeros((BAND, hidden_channels), BF16)
    for buf in (hall, pall):
        for a in range(3):
            for b in range(3):
                if a != b:
                    where = BAND * b if b < a else CELLS + BAND * (b - 1)
                    buf[pl.ds(where, BAND), pl.ds(a * hidden_channels, hidden_channels)] = pad
    first.wait_recv()
    first.borders((f3, g3), channels)

    def hidden_part(i, carry):
        here = rows_of(i, BLOCK)
        pre = jnp.zeros((BLOCK, hidden_channels), F32)
        g_hidden = jnp.zeros((BLOCK, hidden_channels), F32)
        for a in range(3):
            window = rows_of(i, BLOCK, BAND * a)
            pre += mm(f3[window, :], w1[a])
            for b in range(3):
                g_hidden += mm(
                    g3[window, pl.ds(b * channels, channels)],
                    w2[2 - a, pl.ds((2 - b) * hidden_channels, hidden_channels), :],
                    NT,
                )
        pre = pre + b1[...]
        m = mfull[here, :]
        bell = 0.5 * (1.0 + lax.erf(pre * ROOT_HALF))
        hidden = (m * (pre * bell)).astype(BF16)
        slope = bell + pre * jnp.exp(-0.5 * pre * pre) * INV_ROOT_TWO_PI
        g_pre = (m * g_hidden * slope).astype(BF16)
        hp[here, pl.ds(0, hidden_channels)] = hidden
        hp[here, pl.ds(hidden_channels, hidden_channels)] = g_pre
        for a in range(3):
            there = rows_of(i, BLOCK, BAND * a)
            lanes = pl.ds(a * hidden_channels, hidden_channels)
            hall[there, lanes] = hidden
            pall[there, lanes] = g_pre
        return carry

    lax.fori_loop(0, BLOCKS, hidden_part, 0)
    second.pack()
    second.start()

    ones = jnp.ones((PART, CELLS), BF16)
    sum_pre = mm(ones, hp[:, pl.ds(hidden_channels, hidden_channels)])
    sum_mixed = mm(ones, fg[:, pl.ds(channels, channels)])
    if fused:
        shard_c, shard_h = channels // n_space, hidden_channels // n_space
        share0, share1 = reductions[0].share, reductions[1].share
        quarter = share0.shape[3]

        def put(share, s, row, value):
            done = 0
            count = value.shape[0]
            while done < count:
                at = row + done
                k, within = at // quarter, at % quarter
                size = min(count - done, quarter - within)
                share[s % 2, s // 2, k, pl.ds(within, size), :] = value[done : done + size]
                done += size

        halves = channels // 128
        rows2 = 9 * shard_h * halves
        for b in range(3):
            sums = mm(hall[...], g3[:, pl.ds((2 - b) * channels, channels)], TN).astype(BF16)
            for a in range(3):
                part = sums[(2 - a) * hidden_channels : (3 - a) * hidden_channels]
                t = 3 * a + b
                for s in range(n_space):
                    for half in range(halves):
                        put(
                            share0,
                            s,
                            (t * halves + half) * shard_h,
                            part[s * shard_h : (s + 1) * shard_h, half * 128 : half * 128 + 128],
                        )
        r, _ = grid2(PART, 128)
        biases = jnp.where(
            r == 0,
            sum_pre,
            jnp.where(r == 1, sum_mixed[:, :128], jnp.where(r == 2, sum_mixed[:, 128:], 0.0)),
        ).astype(BF16)
        for s in range(n_space):
            put(share0, s, rows2, biases)
            left = n_snap * quarter - rows2 - PART
            if left:
                put(share0, s, rows2 + PART, jnp.zeros((left, 128), BF16))
        reductions[0].start_a()

        rows1 = 9 * shard_c
        for b in range(3):
            sums = mm(pall[...], f3[:, pl.ds(b * channels, channels)], TN)
            for a in range(3):
                part = sums[a * hidden_channels : (a + 1) * hidden_channels].T.astype(BF16)
                t = 3 * a + b
                for s in range(n_space):
                    put(share1, s, t * shard_c, part[s * shard_c : (s + 1) * shard_c])
        for s in range(n_space):
            left = n_snap * quarter - rows1
            if left:
                put(share1, s, rows1, jnp.zeros((left, 128), BF16))
        reductions[1].start_a()
        reductions[0].start_b()
    else:
        for b in range(3):
            sums = mm(hall[...], g3[:, pl.ds((2 - b) * channels, channels)], TN)
            for a in range(3):
                gw2[3 * a + b] = sums[(2 - a) * hidden_channels : (3 - a) * hidden_channels]
            sums = mm(pall[...], f3[:, pl.ds(b * channels, channels)], TN)
            for a in range(3):
                gw1[3 * a + b] = sums[a * hidden_channels : (a + 1) * hidden_channels].T
        gb1[...] = sum_pre[0:1]
        gb2[...] = sum_mixed[0:1]

    second.interior((h3, p3), hidden_channels)
    second.wait_recv()
    second.borders((h3, p3), hidden_channels)

    if fused:
        reductions[1].start_b()

    def out_part(i, carry):
        here = rows_of(i, BLOCK)
        mixed = jnp.zeros((BLOCK, channels), F32)
        for a in range(3):
            mixed += mm(h3[rows_of(i, BLOCK, BAND * a), :], w2[a])
        mixed = mixed + b2[...]
        m = mfull[here, :]
        for half in range(channels // 128):
            lanes = pl.ds(half * 128, 128)
            field_out[here, lanes] = (
                field[here, lanes].astype(F32) + m * mixed[:, half * 128 : half * 128 + 128]
            ).astype(BF16)
        return carry

    def grad_part(i, carry):
        here = rows_of(i, BLOCK)
        total = jnp.zeros((BLOCK, channels), F32)
        for a in range(3):
            window = rows_of(i, BLOCK, BAND * a)
            for b in range(3):
                total += mm(
                    p3[window, pl.ds(b * hidden_channels, hidden_channels)],
                    w1[2 - a, pl.ds((2 - b) * channels, channels), :],
                    NT,
                )
        grad_field[here, :] = (cot[here, :].astype(F32) + total).astype(BF16)
        return carry

    lax.fori_loop(0, BLOCKS, out_part, 0)
    if fused:
        reductions[0].start_c()
    lax.fori_loop(0, BLOCKS, grad_part, 0)
    if fused:
        reductions[0].start_d()
        reductions[1].start_c()
        reductions[0].finish(scale, whole)

        def get(row, count):
            pieces = []
            done = 0
            while done < count:
                at = row + done
                k, within = at // quarter, at % quarter
                size = min(count - done, quarter - within)
                pieces.append(whole[k, pl.ds(within, size), :])
                done += size
            return pieces[0] if len(pieces) == 1 else jnp.concatenate(pieces, axis=0)

        for t in range(9):
            for half in range(halves):
                gw2[t, :, pl.ds(half * 128, 128)] = get((t * halves + half) * shard_h, shard_h)
        tail = get(rows2, PART)
        r, c = grid2(128, shard_h)
        pick = jnp.where(r == c + me * shard_h, 1.0, 0.0)
        gb1[...] = jnp.dot(
            tail, pick, preferred_element_type=F32, precision=lax.Precision.HIGHEST
        )[0:1]
        picked = jnp.zeros((PART, shard_c), F32)
        for half in range(halves):
            r, c = grid2(128, shard_c)
            pick = jnp.where(r + half * 128 == c + me * shard_c, 1.0, 0.0)
            picked = picked + jnp.where(
                lax.broadcasted_iota(jnp.int32, (PART, shard_c), 0) == 1 + half,
                jnp.dot(tail, pick, preferred_element_type=F32, precision=lax.Precision.HIGHEST),
                0.0,
            )
        gb2[...] = jnp.sum(picked, axis=0, keepdims=True)

        reductions[1].start_d()
        reductions[1].finish(scale, whole)
        for t in range(9):
            gw1[t] = get(t * shard_c, shard_c)
        for red in reductions:
            red.wait_send()
    first.wait_send()
    second.wait_send()


def local(field_in, ocean_mask, cotangent, w_first, b_first, w_second, b_second):
    n_space, n_snap = lax.axis_size("space"), lax.axis_size("snap")
    tall, wide, channels = field_in.shape[2:]
    hidden_channels = w_first.shape[3]
    total = field_in.shape[0] * n_snap * n_space * tall * wide
    scale = 1.0 / math.sqrt(float(total))
    cells = tall * wide
    shard_c, shard_h = channels // n_space, hidden_channels // n_space
    fused = shard_c % 16 == 0 and shard_h % 16 == 0

    def halo_scratch(width):
        return [
            pltpu.VMEM((cells, width), BF16),
            pltpu.VMEM((2, EDGE, width), BF16),
            pltpu.VMEM((4, BAND, width), BF16),
            pltpu.VMEM((4, PART, width), BF16),
            pltpu.VMEM((cells + 2 * BAND, 3 * width // 2), BF16),
            pltpu.VMEM((cells + 2 * BAND, 3 * width // 2), BF16),
            pltpu.SemaphoreType.DMA((8,)),
            pltpu.SemaphoreType.DMA((8,)),
        ]

    scratch = halo_scratch(2 * channels) + halo_scratch(2 * hidden_channels)
    scratch += [
        pltpu.VMEM((cells, 128), F32),
        pltpu.VMEM((cells + 2 * BAND, 3 * hidden_channels), BF16),
        pltpu.VMEM((cells + 2 * BAND, 3 * hidden_channels), BF16),
    ]
    if fused:
        chips = n_space // 2
        need = max(9 * shard_c * hidden_channels // 128, 9 * shard_h * channels // 128 + PART)
        quarter = -(-need // (PART * n_snap)) * PART
        for _ in range(2):
            piece = (quarter, 128)
            scratch += [
                pltpu.VMEM((2, chips, n_snap) + piece, BF16),
                pltpu.VMEM((chips, n_snap) + piece, BF16),
                pltpu.VMEM((n_snap, chips) + piece, BF16),
                pltpu.VMEM((n_snap - 1, chips) + piece, BF16),
                pltpu.VMEM((chips,) + piece, BF16),
                pltpu.VMEM((chips - 1,) + piece, BF16),
                pltpu.VMEM(piece, BF16),
                pltpu.VMEM((n_snap - 1,) + piece, BF16),
                pltpu.SemaphoreType.DMA,
                pltpu.SemaphoreType.DMA,
                pltpu.SemaphoreType.DMA((n_snap - 1,)),
                pltpu.SemaphoreType.DMA((n_snap - 1,)),
                pltpu.SemaphoreType.DMA((chips - 1,)),
                pltpu.SemaphoreType.DMA((chips - 1,)),
                pltpu.SemaphoreType.DMA((n_snap - 1,)),
                pltpu.SemaphoreType.DMA((n_snap - 1,)),
            ]
        scratch += [pltpu.VMEM((n_snap, quarter, 128), F32)]
        grads = [
            jax.ShapeDtypeStruct((9, shard_c, hidden_channels), F32),
            jax.ShapeDtypeStruct((9, shard_h, channels), F32),
            jax.ShapeDtypeStruct((1, shard_h), F32),
            jax.ShapeDtypeStruct((1, shard_c), F32),
        ]
    else:
        grads = [
            jax.ShapeDtypeStruct((9, channels, hidden_channels), F32),
            jax.ShapeDtypeStruct((9, hidden_channels, channels), F32),
            jax.ShapeDtypeStruct((1, hidden_channels), F32),
            jax.ShapeDtypeStruct((1, channels), F32),
        ]
    vmem = pl.BlockSpec(memory_space=pltpu.VMEM)
    field_out, grad_field, gw1, gw2, gb1, gb2 = pl.pallas_call(
        functools.partial(kernel, n_space, n_snap, fused, scale),
        out_shape=[jax.ShapeDtypeStruct((cells, channels), BF16)] * 2 + grads,
        in_specs=[vmem] * 7,
        out_specs=[vmem] * 6,
        scratch_shapes=scratch,
        compiler_params=pltpu.CompilerParams(
            collective_id=0, has_side_effects=True, vmem_limit_bytes=48 * 1024 * 1024
        ),
    )(
        field_in.reshape(cells, channels),
        ocean_mask.reshape(tall, wide),
        cotangent.reshape(cells, channels),
        w_first.reshape(3, 3 * channels, hidden_channels),
        b_first.reshape(1, hidden_channels),
        w_second.reshape(3, 3 * hidden_channels, channels),
        b_second.reshape(1, channels),
    )
    whole_shape = field_in.shape
    if not fused:
        sums = (
            lax.psum_scatter(gw1, "space", scatter_dimension=1, tiled=True),
            lax.psum_scatter(gw2, "space", scatter_dimension=1, tiled=True),
            lax.psum_scatter(gb1[0], "space", scatter_dimension=0, tiled=True),
            lax.psum_scatter(gb2[0], "space", scatter_dimension=0, tiled=True),
        )
        gw1, gw2, gb1, gb2 = [value * scale for value in lax.psum(sums, "snap")]
    return (
        field_out.reshape(whole_shape),
        grad_field.reshape(whole_shape),
        gw1.reshape(3, 3, shard_c, hidden_channels),
        gw2.reshape(3, 3, shard_h, channels),
        gb1.reshape(shard_h),
        gb2.reshape(shard_c),
    )


def solution(mesh):
    placed = (
        P("snap", "space", None, None, None),
        P("space", None, None),
        P("snap", "space", None, None, None),
        P(),
        P(),
        P(),
        P(),
    )
    return jax.shard_map(
        local,
        mesh=mesh,
        in_specs=placed,
        out_specs=(
            P("snap", "space", None, None, None),
            P("snap", "space", None, None, None),
            P(None, None, "space", None),
            P(None, None, "space", None),
            P("space"),
            P("space"),
        ),
        check_vma=False,
    )
```

time: 169 us -> 48.1 us (0.28)
  waiting for transfers between devices: 70.8 us -> 0 us
  Pallas kernels: 0 us -> 37.5 us
  starting transfers between devices: 24.7 us -> 0 us
  blocking collectives: 23.9 us -> 0 us
  between operations: 15.8 us -> 0.67 us
  other arithmetic: 14.5 us -> 0 us
  matrix products: 11.4 us -> 0 us
  local copies, waits for them, and re-layouts: 7.18 us -> 9.52 us
    psum x1 -> x0, waiting for transfers between devices: 43.6 us -> none  [local(): summed = lax.psum((shares[0], shares[1], shares[2], shares[3]), 'snap')]
    pallas_call x0 -> x1, Pallas kernels: none -> 37.5 us  [local(): pl.pallas_call(functools.partial(kernel, n_space, n_snap, fused, scale),...]
    ppermute x16 -> x0, starting transfers between devices: 24.4 us -> none  [from_behind(): lax.ppermute(array, axis, [(i, (i + by) % length) for i in range(length)])]
    reduce_scatter x2 -> x0, waiting for transfers between devices: 17.9 us -> none  [the longest x1 17.9 us: local(): lax.psum_scatter(grad_wb, 'space', scatter_dimension=2, tiled=True)]
    unnamed x1 -> x0, blocking collectives: 13.9 us -> none
    psum x1 -> x0, blocking collectives: 10 us -> none  [local(): summed = lax.psum((shares[0], shares[1], shares[2], shares[3]), 'snap')]
    ppermute x16 -> x0, waiting for transfers between devices: 9.21 us -> none  [from_behind(): lax.ppermute(array, axis, [(i, (i + by) % length) for i in range(length)])]
    unnamed x25 -> x20, local copies, waits for them, and re-layouts: 3.25 us -> 9.52 us
  transfers between devices with their start and end apart: 19 -> 0, of which waited for: 5 -> 0; matrix products, arithmetic and copies ran while one was open for 11% -> 0% of each run, Pallas kernels for 0% -> 0%
where the time goes in v1:
time: 48.1 us; the launch traced here: 47.7 us
  Pallas kernels  37.5 us (78%)
  local copies, waits for them, and re-layouts  9.52 us (20%)
  between operations  0.67 us (1%)
    pallas_call x1, Pallas kernels, local(): pl.pallas_call(functools.partial(kernel, n_space, n_snap, fused, scale),...  37.5 us
    unnamed x20, local copies, waits for them, and re-layouts  9.52 us

profile of v1, /device:TPU:0, one launch (start us, length us, event | category | flops | bytes accessed | tf_op | source)
XLA Modules:
  0.0 47.7 jit_solution(2530051175236291641)
XLA Ops:
  0.6 0.0 copy-start.5
  0.6 0.0 copy-start.6
  0.7 0.7 %copy-done.5 = f32[256]{0:T(256)S(1)} copy-done((f32[256]{0:T(256)S(1)}, f32[256]{0:T(256)}, u32[]{:S(2)}) %copy-start.5) | copy-done | bytes 1048
  1.3 0.0 copy-done.6
  1.3 0.0 copy-start
  1.3 1.1 %copy-done = bf16[3,3,256,128]{3,2,1,0:T(8,128)(2,1)S(1)} copy-done((bf16[3,3,256,128]{3,2,1,0:T(8,128)(2,1)S(1)}, bf16[3,3,256,128]{3,2,1,0:T(8,128)(2,1)}, u32[]{:S(2)}) %copy-start) | copy-done | bytes 589848
  2.4 0.0 copy-start.1
  2.4 1.1 %copy-done.1 = bf16[3,3,128,256]{3,2,1,0:T(8,128)(2,1)S(1)} copy-done((bf16[3,3,128,256]{3,2,1,0:T(8,128)(2,1)S(1)}, bf16[3,3,128,256]{3,2,1,0:T(8,128)(2,1)}, u32[]{:S(2)}) %copy-start.1) | copy-done | bytes 589848
  3.4 0.0 copy-start.2
  3.4 1.0 %copy-done.2 = bf16[1,1,32,32,256]{4,3,2,1,0:T(8,128)(2,1)S(1)} copy-done((bf16[1,1,32,32,256]{4,3,2,1,0:T(8,128)(2,1)S(1)}, bf16[1,1,32,32,256]{4,3,2,1,0:T(8,128)(2,1)}, u32[]{:S(2)}) %copy-start.2) | copy-done | bytes 524312
  4.5 0.0 copy-start.3
  4.5 1.0 %copy-done.3 = bf16[1,1,32,32,256]{4,3,2,1,0:T(8,128)(2,1)S(1)} copy-done((bf16[1,1,32,32,256]{4,3,2,1,0:T(8,128)(2,1)S(1)}, bf16[1,1,32,32,256]{4,3,2,1,0:T(8,128)(2,1)}, u32[]{:S(2)}) %copy-start.3) | copy-done | bytes 524312
  5.5 0.0 copy-start.4
  5.5 0.7 %copy-done.4 = s32[1,32,32]{2,1,0:T(8,128)S(1)} copy-done((s32[1,32,32]{2,1,0:T(8,128)S(1)}, s32[1,32,32]{2,1,0:T(8,128)}, u32[]{:S(2)}) %copy-start.4) | copy-done | bytes 4120
  6.2 37.5 %shard_map.118 = (bf16[1024,256]{1,0:T(8,128)(2,1)S(1)}, bf16[1024,256]{1,0:T(8,128)(2,1)S(1)}, f32[9,32,128]{2,1,0:T(8,128)S(1)}, f32[9,16,256]{2,1,0:T(8,128)S...) custom-call(bf16[1024,256]{1,0:T(8,128)(2,1)S(1)} %bitcast.15, s32[32,32]{1,0:T(8,128)S(1)} %bitcast.21, ...), custom_call_target="tpu_custom_call" | custom-call | tf_op jit(solution)/shard_map/pallas_call | solution.py:664
  43.8 0.8 %copy.19 = bf16[1,1,32,32,256]{4,3,2,1,0:T(8,128)(2,1)} copy(bf16[1,1,32,32,256]{4,3,2,1,0:T(8,128)(2,1)S(1)} %bitcast.18) | data formatting | bytes 1048576
  44.6 0.8 %copy.20 = bf16[1,1,32,32,256]{4,3,2,1,0:T(8,128)(2,1)} copy(bf16[1,1,32,32,256]{4,3,2,1,0:T(8,128)(2,1)S(1)} %bitcast.17) | data formatting | bytes 1048576
  45.4 0.7 %copy.21 = f32[3,3,32,128]{3,2,1,0:T(8,128)} copy(f32[3,3,32,128]{3,2,1,0:T(8,128)S(1)} %bitcast.20) | data formatting | bytes 294912
  46.0 0.7 %copy.22 = f32[3,3,16,256]{3,2,1,0:T(8,128)} copy(f32[3,3,16,256]{3,2,1,0:T(8,128)S(1)} %bitcast.19) | data formatting | bytes 294912
  46.7 0.5 %copy.23 = f32[16]{0:T(128)} copy(f32[16]{0:T(128)S(1)} %bitcast.25) | data formatting | bytes 128
  47.2 0.5 %copy.24 = f32[32]{0:T(128)} copy(f32[32]{0:T(128)S(1)} %bitcast.24) | data formatting | bytes 256
Async XLA Ops:
  0.6 0.7 %copy-start.5 = (f32[256]{0:T(256)S(1)}, f32[256]{0:T(256)}, u32[]{:S(2)}) copy-start(f32[256]{0:T(256)} %param.13) | copy-start | bytes 3076
  0.6 0.7 %copy-start.6 = (f32[128]{0:T(128)S(1)}, f32[128]{0:T(128)}, u32[]{:S(2)}) copy-start(f32[128]{0:T(128)} %param.11) | copy-start | bytes 1540
  1.3 1.1 %copy-start = (bf16[3,3,256,128]{3,2,1,0:T(8,128)(2,1)S(1)}, bf16[3,3,256,128]{3,2,1,0:T(8,128)(2,1)}, u32[]{:S(2)}) copy-start(bf16[3,3,256,128]{3,2,1,0:T(8,128)(2,1)} %param.10) | copy-start | bytes 1769476
  2.4 1.1 %copy-start.1 = (bf16[3,3,128,256]{3,2,1,0:T(8,128)(2,1)S(1)}, bf16[3,3,128,256]{3,2,1,0:T(8,128)(2,1)}, u32[]{:S(2)}) copy-start(bf16[3,3,128,256]{3,2,1,0:T(8,128)(2,1)} %param.12) | copy-start | bytes 1769476
  3.4 1.0 %copy-start.2 = (bf16[1,1,32,32,256]{4,3,2,1,0:T(8,128)(2,1)S(1)}, bf16[1,1,32,32,256]{4,3,2,1,0:T(8,128)(2,1)}, u32[]{:S(2)}) copy-start(bf16[1,1,32,32,256]{4,3,2,1,0:T(8,128)(2,1)} %param.7) | copy-start | bytes 1572868
  4.5 1.0 %copy-start.3 = (bf16[1,1,32,32,256]{4,3,2,1,0:T(8,128)(2,1)S(1)}, bf16[1,1,32,32,256]{4,3,2,1,0:T(8,128)(2,1)}, u32[]{:S(2)}) copy-start(bf16[1,1,32,32,256]{4,3,2,1,0:T(8,128)(2,1)} %param.9) | copy-start | bytes 1572868
  5.5 0.7 %copy-start.4 = (s32[1,32,32]{2,1,0:T(8,128)S(1)}, s32[1,32,32]{2,1,0:T(8,128)}, u32[]{:S(2)}) copy-start(s32[1,32,32]{2,1,0:T(8,128)} %param.8) | copy-start | bytes 12292

commit v2 on v1

--- a/solution.py
+++ b/solution.py
@@ -25,6 +25,7 @@
 BAND = 2 * WIDE
 BLOCK = 8 * WIDE
 BLOCKS = CELLS // BLOCK
+STEP = CELLS // 2
 EDGE = 2 * TALL
 PART = 16
 
@@ -311,12 +312,25 @@
         del refs[:count]
         return got
 
-    field, mask, cot, w1, b1, w2, b2 = take(7)
-    field_out, grad_field, gw1, gw2, gb1, gb2 = take(6)
+    sources = take(7)
+    field_dst, grad_dst, gw1, gw2, gb1, gb2 = take(6)
     fg, fg_packs, fg_bands, fg_corners, f3, g3, fg_send, fg_recv = take(8)
     hp, hp_packs, hp_bands, hp_corners, h3, p3, hp_send, hp_recv = take(8)
-    mfull, hall, pall = take(3)
-    channels, hidden_channels = field.shape[1], hp.shape[1] // 2
+    mfull, hall, pall, w1t, w2t = take(5)
+    mask, cot, w1, b1, w2, b2, load_sem = take(7)
+    field_out, grad_field, store_sem = take(3)
+    stores = [
+        pltpu.make_async_copy(field_out, field_dst, store_sem.at[0]),
+        pltpu.make_async_copy(grad_field, grad_dst, store_sem.at[1]),
+    ]
+    channels, hidden_channels = cot.shape[1], hp.shape[1] // 2
+    field = fg.at[:, pl.ds(0, channels)]
+    loads = [
+        pltpu.make_async_copy(src, dst, load_sem.at[n])
+        for n, (src, dst) in enumerate(zip(sources, (field, mask, cot, w1, b1, w2, b2)))
+    ]
+    for n in (1, 2, 0, 3, 5, 4, 6):
+        loads[n].start()
 
     me = lax.axis_index("space")
     position = lax.rem(me + 1, n_space)
@@ -346,8 +360,6 @@
 
     first = Halo(geometry, fg, fg_packs, fg_bands, fg_corners, fg_send, fg_recv)
     second = Halo(geometry, hp, hp_packs, hp_bands, hp_corners, hp_send, hp_recv)
-    first.clear_missing()
-    second.clear_missing()
 
     barrier = pltpu.get_barrier_semaphore()
     expected = jnp.int32(0)
@@ -373,6 +385,11 @@
             )
         expected = expected + (1 + n_snap - 1 + n_space // 2 - 1)
 
+    first.clear_missing()
+    second.clear_missing()
+    for n in (1, 2, 0):
+        loads[n].wait()
+
     mask_bits = mask[...].astype(F32).astype(BF16)
 
     def prepare(i, carry):
@@ -383,7 +400,6 @@
         one = jnp.where((r & (WIDE - 1)) == x, lines_of, 0.0).astype(BF16)
         m = mm(one, jnp.ones((WIDE, 128), BF16))
         mfull[here, :] = m
-        fg[here, pl.ds(0, channels)] = field[here, :]
         for half in range(channels // 128):
             lanes = pl.ds(half * 128, 128)
             fg[here, pl.ds(channels + half * 128, 128)] = (
@@ -396,6 +412,16 @@
     pl.semaphore_wait(barrier, expected)
     first.start()
     first.interior((f3, g3), channels)
+    for n in (3, 4, 5, 6):
+        loads[n].wait()
+    for a in range(3):
+        for b in range(3):
+            w2t[a, pl.ds(b * channels, channels), :] = w2[
+                2 - a, pl.ds((2 - b) * hidden_channels, hidden_channels), :
+            ].T
+            w1t[a, pl.ds(b * hidden_channels, hidden_channels), :] = w1[
+                2 - a, pl.ds((2 - b) * channels, channels), :
+            ].T
     pad = jnp.zeros((BAND, hidden_channels), BF16)
     for buf in (hall, pall):
         for a in range(3):
@@ -407,18 +433,13 @@
     first.borders((f3, g3), channels)
 
     def hidden_part(i, carry):
-        here = rows_of(i, BLOCK)
-        pre = jnp.zeros((BLOCK, hidden_channels), F32)
-        g_hidden = jnp.zeros((BLOCK, hidden_channels), F32)
+        here = rows_of(i, STEP)
+        pre = jnp.zeros((STEP, hidden_channels), F32)
+        g_hidden = jnp.zeros((STEP, hidden_channels), F32)
         for a in range(3):
-            window = rows_of(i, BLOCK, BAND * a)
+            window = rows_of(i, STEP, BAND * a)
             pre += mm(f3[window, :], w1[a])
-            for b in range(3):
-                g_hidden += mm(
-                    g3[window, pl.ds(b * channels, channels)],
-                    w2[2 - a, pl.ds((2 - b) * hidden_channels, hidden_channels), :],
-                    NT,
-                )
+            g_hidden += mm(g3[window, :], w2t[a])
         pre = pre + b1[...]
         m = mfull[here, :]
         bell = 0.5 * (1.0 + lax.erf(pre * ROOT_HALF))
@@ -428,13 +449,13 @@
         hp[here, pl.ds(0, hidden_channels)] = hidden
         hp[here, pl.ds(hidden_channels, hidden_channels)] = g_pre
         for a in range(3):
-            there = rows_of(i, BLOCK, BAND * a)
+            there = rows_of(i, STEP, BAND * a)
             lanes = pl.ds(a * hidden_channels, hidden_channels)
             hall[there, lanes] = hidden
             pall[there, lanes] = g_pre
         return carry
 
-    lax.fori_loop(0, BLOCKS, hidden_part, 0)
+    lax.fori_loop(0, CELLS // STEP, hidden_part, 0)
     second.pack()
     second.start()
 
@@ -458,8 +479,9 @@
 
         halves = channels // 128
         rows2 = 9 * shard_h * halves
+        all_sums = mm(hall[...], g3[...], TN).astype(BF16)
         for b in range(3):
-            sums = mm(hall[...], g3[:, pl.ds((2 - b) * channels, channels)], TN).astype(BF16)
+            sums = all_sums[:, (2 - b) * channels : (3 - b) * channels]
             for a in range(3):
                 part = sums[(2 - a) * hidden_channels : (3 - a) * hidden_channels]
                 t = 3 * a + b
@@ -485,8 +507,9 @@
         reductions[0].start_a()
 
         rows1 = 9 * shard_c
+        all_sums = mm(pall[...], f3[...], TN)
         for b in range(3):
-            sums = mm(pall[...], f3[:, pl.ds(b * channels, channels)], TN)
+            sums = all_sums[:, b * channels : (b + 1) * channels]
             for a in range(3):
                 part = sums[a * hidden_channels : (a + 1) * hidden_channels].T.astype(BF16)
                 t = 3 * a + b
@@ -517,10 +540,10 @@
         reductions[1].start_b()
 
     def out_part(i, carry):
-        here = rows_of(i, BLOCK)
-        mixed = jnp.zeros((BLOCK, channels), F32)
+        here = rows_of(i, STEP)
+        mixed = jnp.zeros((STEP, channels), F32)
         for a in range(3):
-            mixed += mm(h3[rows_of(i, BLOCK, BAND * a), :], w2[a])
+            mixed += mm(h3[rows_of(i, STEP, BAND * a), :], w2[a])
         mixed = mixed + b2[...]
         m = mfull[here, :]
         for half in range(channels // 128):
@@ -531,23 +554,19 @@
         return carry
 
     def grad_part(i, carry):
-        here = rows_of(i, BLOCK)
-        total = jnp.zeros((BLOCK, channels), F32)
+        here = rows_of(i, STEP)
+        total = jnp.zeros((STEP, channels), F32)
         for a in range(3):
-            window = rows_of(i, BLOCK, BAND * a)
-            for b in range(3):
-                total += mm(
-                    p3[window, pl.ds(b * hidden_channels, hidden_channels)],
-                    w1[2 - a, pl.ds((2 - b) * channels, channels), :],
-                    NT,
-                )
+            total += mm(p3[rows_of(i, STEP, BAND * a), :], w1t[a])
         grad_field[here, :] = (cot[here, :].astype(F32) + total).astype(BF16)
         return carry
 
-    lax.fori_loop(0, BLOCKS, out_part, 0)
+    lax.fori_loop(0, CELLS // STEP, out_part, 0)
+    stores[0].start()
     if fused:
         reductions[0].start_c()
-    lax.fori_loop(0, BLOCKS, grad_part, 0)
+    lax.fori_loop(0, CELLS // STEP, grad_part, 0)
+    stores[1].start()
     if fused:
         reductions[0].start_d()
         reductions[1].start_c()
@@ -592,6 +611,19 @@
             red.wait_send()
     first.wait_send()
     second.wait_send()
+    for c in stores:
+        c.wait()
+
+
+def store_all(*refs):
+    sem = refs[-1]
+    copies = [
+        pltpu.make_async_copy(refs[n], refs[6 + n], sem.at[n]) for n in range(6)
+    ]
+    for c in copies:
+        c.start()
+    for c in copies:
+        c.wait()
 
 
 def local(field_in, ocean_mask, cotangent, w_first, b_first, w_second, b_second):
@@ -621,6 +653,18 @@
         pltpu.VMEM((cells, 128), F32),
         pltpu.VMEM((cells + 2 * BAND, 3 * hidden_channels), BF16),
         pltpu.VMEM((cells + 2 * BAND, 3 * hidden_channels), BF16),
+        pltpu.VMEM((3, 3 * hidden_channels, channels), BF16),
+        pltpu.VMEM((3, 3 * channels, hidden_channels), BF16),
+        pltpu.VMEM((tall, wide), jnp.int32),
+        pltpu.VMEM((cells, channels), BF16),
+        pltpu.VMEM((3, 3 * channels, hidden_channels), BF16),
+        pltpu.VMEM((1, hidden_channels), F32),
+        pltpu.VMEM((3, 3 * hidden_channels, channels), BF16),
+        pltpu.VMEM((1, channels), F32),
+        pltpu.SemaphoreType.DMA((7,)),
+        pltpu.VMEM((cells, channels), BF16),
+        pltpu.VMEM((cells, channels), BF16),
+        pltpu.SemaphoreType.DMA((2,)),
     ]
     if fused:
         chips = n_space // 2
@@ -661,14 +705,14 @@
             jax.ShapeDtypeStruct((1, channels), F32),
         ]
     vmem = pl.BlockSpec(memory_space=pltpu.VMEM)
-    field_out, grad_field, gw1, gw2, gb1, gb2 = pl.pallas_call(
+    results = pl.pallas_call(
         functools.partial(kernel, n_space, n_snap, fused, scale),
         out_shape=[jax.ShapeDtypeStruct((cells, channels), BF16)] * 2 + grads,
-        in_specs=[vmem] * 7,
-        out_specs=[vmem] * 6,
+        in_specs=[pl.BlockSpec(memory_space=pl.ANY)] * 7,
+        out_specs=[pl.BlockSpec(memory_space=pl.ANY)] * 2 + [vmem] * 4,
         scratch_shapes=scratch,
         compiler_params=pltpu.CompilerParams(
-            collective_id=0, has_side_effects=True, vmem_limit_bytes=48 * 1024 * 1024
+            collective_id=0, has_side_effects=True, vmem_limit_bytes=60 * 1024 * 1024
         ),
     )(
         field_in.reshape(cells, channels),
@@ -679,6 +723,13 @@
         w_second.reshape(3, 3 * hidden_channels, channels),
         b_second.reshape(1, channels),
     )
+    field_out, grad_field, gw1, gw2, gb1, gb2 = pl.pallas_call(
+        store_all,
+        out_shape=[jax.ShapeDtypeStruct(value.shape, value.dtype) for value in results],
+        in_specs=[pl.BlockSpec(memory_space=pl.ANY)] * 6,
+        out_specs=[pl.BlockSpec(memory_space=pl.ANY)] * 6,
+        scratch_shapes=[pltpu.SemaphoreType.DMA((6,))],
+    )(*results)
     whole_shape = field_in.shape
     if not fused:
         sums = (

time: 48.1 us -> 81.5 us (1.69)
  Pallas kernels: 37.5 us -> 80.6 us
  local copies, waits for them, and re-layouts: 9.52 us -> 0 us
    pallas_call x0 -> x1, Pallas kernels: none -> 41.9 us  [local(): pl.pallas_call(store_all, out_shape=[jax.ShapeDtypeStruct(value.shape, va...]
    unnamed x20 -> x0, local copies, waits for them, and re-layouts: 9.52 us -> none
    pallas_call x1, Pallas kernels: 37.5 us -> 38.7 us  [local(): pl.pallas_call(functools.partial(kernel, n_space, n_snap, fused, scale),...]
where the time goes in v2:
time: 81.5 us; the launch traced here: 81.2 us
  Pallas kernels  80.6 us (99%)
    pallas_call x1, Pallas kernels, local(): pl.pallas_call(store_all, out_shape=[jax.ShapeDtypeStruct(value.shape, va...  41.9 us
    pallas_call x1, Pallas kernels, local(): pl.pallas_call(functools.partial(kernel, n_space, n_snap, fused, scale),...  38.7 us

profile of v2, /device:TPU:0, one launch (start us, length us, event | category | flops | bytes accessed | tf_op | source)
XLA Modules:
  0.0 81.2 jit_solution(5359139353507625132)
XLA Ops:
  0.6 38.7 %shard_map.118 = (bf16[1024,256]{1,0:T(8,128)(2,1)}, bf16[1024,256]{1,0:T(8,128)(2,1)}, f32[9,32,128]{2,1,0:T(8,128)}, f32[9,16,256]{2,1,0:T(8,128)}, f32[1,16]{1,0:T(1,128)}, /*index=5*/f32[1,32]{1,0:T(1,128)}) custom-call(bf16[1024,256]{1,0:T(8,128)(2,1)} %bitcast.15, s32[32,32]{1,0:T(8,128)} %bitcast.17, bf16[1024,256]{1,0:T(8,128)(2,1)} %bitcast.16, ...), custom_call_target="tpu_custom_call" | custom-call | tf_op jit(solution)/shard_map/pallas_call | solution.py:708
  39.3 41.9 %shard_map.119 = (bf16[1024,256]{1,0:T(8,128)(2,1)}, bf16[1024,256]{1,0:T(8,128)(2,1)}, f32[9,32,128]{2,1,0:T(8,128)}, f32[9,16,256]{2,1,0:T(8,128)}, f32[1,16]{1,0:T(1,128)}, /*index=5*/f32[1,32]{1,0:T(1,128)}) custom-call(bf16[1024,256]{1,0:T(8,128)(2,1)} %get-tuple-element.18.refs_0_, bf16[1024,256]{1,0:T(8,128)(2,1)} %get-tuple-element.19.refs_1_, ...), custom_call_target="tpu_custom_call" | custom-call | tf_op jit(solution)/shard_map/pallas_call | solution.py:726

commit v3 on v2

--- a/solution.py
+++ b/solution.py
@@ -154,39 +154,30 @@
             def _():
                 self.copies[d].wait_send()
 
-    def interior(self, outs, width):
+    def interior(self, out):
+        width = self.own.shape[1]
         from_left, from_right = shift_left_source(BLOCK), shift_right_source(BLOCK)
 
         def body(i, carry):
             cells = self.own[rows_of(i, BLOCK), :]
             there = rows_of(i, BLOCK, BAND)
-            shifted = (
-                mm(from_left, cells).astype(BF16),
-                cells,
-                mm(from_right, cells).astype(BF16),
-            )
-            for b in range(3):
-                for n, out in enumerate(outs):
-                    out[there, pl.ds(b * width, width)] = shifted[b][
-                        :, n * width : (n + 1) * width
-                    ]
+            out[there, pl.ds(0, width)] = mm(from_left, cells).astype(BF16)
+            out[there, pl.ds(width, width)] = cells
+            out[there, pl.ds(2 * width, width)] = mm(from_right, cells).astype(BF16)
             return carry
 
         lax.fori_loop(0, BLOCKS, body, 0)
 
-    def borders(self, outs, width):
+    def borders(self, out):
+        width = self.own.shape[1]
         into_left, into_right = left_insert(BLOCK, 0), right_insert(BLOCK, 0)
 
         def body(i, carry):
             there = rows_of(i, BLOCK, BAND)
-            left = mm(into_left, self.bands[LEFT, rows_of(i, PART), :]).astype(BF16)
-            right = mm(into_right, self.bands[RIGHT, rows_of(i, PART), :]).astype(BF16)
-            for n, out in enumerate(outs):
-                mine = slice(n * width, (n + 1) * width)
-                out[there, pl.ds(0, width)] = out[there, pl.ds(0, width)] + left[:, mine]
-                out[there, pl.ds(2 * width, width)] = (
-                    out[there, pl.ds(2 * width, width)] + right[:, mine]
-                )
+            for into, side, b in ((into_left, LEFT, 0), (into_right, RIGHT, 2)):
+                lanes = pl.ds(b * width, width)
+                edge = mm(into, self.bands[side, rows_of(i, PART), :]).astype(BF16)
+                out[there, lanes] = out[there, lanes] + edge
             return carry
 
         lax.fori_loop(0, BLOCKS, body, 0)
@@ -196,22 +187,14 @@
             (DOWN, 0, CELLS + BAND, (DOWN_LEFT, DOWN_RIGHT)),
         ):
             cells = self.bands[band]
-            shifted = (
-                (
-                    mm(from_left, cells)
-                    + mm(left_insert(BAND, first), self.corners[side[0] - 4])
-                ).astype(BF16),
-                cells,
-                (
-                    mm(from_right, cells)
-                    + mm(right_insert(BAND, first), self.corners[side[1] - 4])
-                ).astype(BF16),
-            )
-            for b in range(3):
-                for n, out in enumerate(outs):
-                    out[pl.ds(where, BAND), pl.ds(b * width, width)] = shifted[b][
-                        :, n * width : (n + 1) * width
-                    ]
+            rows = pl.ds(where, BAND)
+            out[rows, pl.ds(0, width)] = (
+                mm(from_left, cells) + mm(left_insert(BAND, first), self.corners[side[0] - 4])
+            ).astype(BF16)
+            out[rows, pl.ds(width, width)] = cells
+            out[rows, pl.ds(2 * width, width)] = (
+                mm(from_right, cells) + mm(right_insert(BAND, first), self.corners[side[1] - 4])
+            ).astype(BF16)
 
 
 class Reduction:
@@ -314,22 +297,22 @@
 
     sources = take(7)
     field_dst, grad_dst, gw1, gw2, gb1, gb2 = take(6)
-    fg, fg_packs, fg_bands, fg_corners, f3, g3, fg_send, fg_recv = take(8)
-    hp, hp_packs, hp_bands, hp_corners, h3, p3, hp_send, hp_recv = take(8)
-    mfull, hall, pall, w1t, w2t = take(5)
+    halo_refs = [take(6) for _ in range(4)]
+    f3, g3, h3, p3 = take(4)
+    mfull, mslope, hall, pall, w1t, w2t = take(6)
     mask, cot, w1, b1, w2, b2, load_sem = take(7)
     field_out, grad_field, store_sem = take(3)
     stores = [
         pltpu.make_async_copy(field_out, field_dst, store_sem.at[0]),
         pltpu.make_async_copy(grad_field, grad_dst, store_sem.at[1]),
     ]
-    channels, hidden_channels = cot.shape[1], hp.shape[1] // 2
-    field = fg.at[:, pl.ds(0, channels)]
+    field, mixed_grad, hidden_ref, pre_grad = [group[0] for group in halo_refs]
+    channels, hidden_channels = cot.shape[1], hidden_ref.shape[1]
     loads = [
         pltpu.make_async_copy(src, dst, load_sem.at[n])
         for n, (src, dst) in enumerate(zip(sources, (field, mask, cot, w1, b1, w2, b2)))
     ]
-    for n in (1, 2, 0, 3, 5, 4, 6):
+    for n in (0, 1, 2, 3, 5, 4, 6):
         loads[n].start()
 
     me = lax.axis_index("space")
@@ -358,8 +341,8 @@
             )
         (whole,) = take(1)
 
-    first = Halo(geometry, fg, fg_packs, fg_bands, fg_corners, fg_send, fg_recv)
-    second = Halo(geometry, hp, hp_packs, hp_bands, hp_corners, hp_send, hp_recv)
+    halos = [Halo(geometry, *group) for group in halo_refs]
+    of_field, of_mixed, of_hidden, of_pre = halos
 
     barrier = pltpu.get_barrier_semaphore()
     expected = jnp.int32(0)
@@ -385,10 +368,14 @@
             )
         expected = expected + (1 + n_snap - 1 + n_space // 2 - 1)
 
-    first.clear_missing()
-    second.clear_missing()
-    for n in (1, 2, 0):
-        loads[n].wait()
+    for halo in halos:
+        halo.clear_missing()
+    loads[0].wait()
+    of_field.pack()
+    pl.semaphore_wait(barrier, expected)
+    of_field.start()
+    loads[1].wait()
+    loads[2].wait()
 
     mask_bits = mask[...].astype(F32).astype(BF16)
 
@@ -402,16 +389,15 @@
         mfull[here, :] = m
         for half in range(channels // 128):
             lanes = pl.ds(half * 128, 128)
-            fg[here, pl.ds(channels + half * 128, 128)] = (
+            mixed_grad[here, lanes] = (
                 cot[here, lanes].astype(F32) * m
             ).astype(BF16)
         return carry
 
     lax.fori_loop(0, BLOCKS, prepare, 0)
-    first.pack()
-    pl.semaphore_wait(barrier, expected)
-    first.start()
-    first.interior((f3, g3), channels)
+    of_mixed.pack()
+    of_mixed.start()
+    of_field.interior(f3)
     for n in (3, 4, 5, 6):
         loads[n].wait()
     for a in range(3):
@@ -429,39 +415,43 @@
                 if a != b:
                     where = BAND * b if b < a else CELLS + BAND * (b - 1)
                     buf[pl.ds(where, BAND), pl.ds(a * hidden_channels, hidden_channels)] = pad
-    first.wait_recv()
-    first.borders((f3, g3), channels)
+    of_mixed.interior(g3)
+    of_field.wait_recv()
+    of_field.borders(f3)
 
     def hidden_part(i, carry):
         here = rows_of(i, STEP)
         pre = jnp.zeros((STEP, hidden_channels), F32)
-        g_hidden = jnp.zeros((STEP, hidden_channels), F32)
         for a in range(3):
-            window = rows_of(i, STEP, BAND * a)
-            pre += mm(f3[window, :], w1[a])
-            g_hidden += mm(g3[window, :], w2t[a])
+            pre += mm(f3[rows_of(i, STEP, BAND * a), :], w1[a])
         pre = pre + b1[...]
         m = mfull[here, :]
         bell = 0.5 * (1.0 + lax.erf(pre * ROOT_HALF))
         hidden = (m * (pre * bell)).astype(BF16)
-        slope = bell + pre * jnp.exp(-0.5 * pre * pre) * INV_ROOT_TWO_PI
-        g_pre = (m * g_hidden * slope).astype(BF16)
-        hp[here, pl.ds(0, hidden_channels)] = hidden
-        hp[here, pl.ds(hidden_channels, hidden_channels)] = g_pre
+        mslope[here, :] = m * (bell + pre * jnp.exp(-0.5 * pre * pre) * INV_ROOT_TWO_PI)
+        hidden_ref[here, :] = hidden
         for a in range(3):
-            there = rows_of(i, STEP, BAND * a)
-            lanes = pl.ds(a * hidden_channels, hidden_channels)
-            hall[there, lanes] = hidden
-            pall[there, lanes] = g_pre
+            hall[rows_of(i, STEP, BAND * a), pl.ds(a * hidden_channels, hidden_channels)] = hidden
         return carry
 
     lax.fori_loop(0, CELLS // STEP, hidden_part, 0)
-    second.pack()
-    second.start()
+    of_hidden.pack()
+    of_hidden.start()
+    of_mixed.wait_recv()
+    of_mixed.borders(g3)
+
+    def pre_grad_part(i, carry):
+        here = rows_of(i, STEP)
+        g_hidden = jnp.zeros((STEP, hidden_channels), F32)
+        for a in range(3):
+            g_hidden += mm(g3[rows_of(i, STEP, BAND * a), :], w2t[a])
+        g_pre = (g_hidden * mslope[here, :]).astype(BF16)
+        pre_grad[here, :] = g_pre
+        for a in range(3):
+            pall[rows_of(i, STEP, BAND * a), pl.ds(a * hidden_channels, hidden_channels)] = g_pre
+        return carry
 
     ones = jnp.ones((PART, CELLS), BF16)
-    sum_pre = mm(ones, hp[:, pl.ds(hidden_channels, hidden_channels)])
-    sum_mixed = mm(ones, fg[:, pl.ds(channels, channels)])
     if fused:
         shard_c, shard_h = channels // n_space, hidden_channels // n_space
         share0, share1 = reductions[0].share, reductions[1].share
@@ -493,20 +483,31 @@
                             (t * halves + half) * shard_h,
                             part[s * shard_h : (s + 1) * shard_h, half * 128 : half * 128 + 128],
                         )
+        for s in range(n_space):
+            left = n_snap * quarter - rows2
+            if left:
+                put(share0, s, rows2, jnp.zeros((left, 128), BF16))
+        reductions[0].start_a()
+
+        lax.fori_loop(0, CELLS // STEP, pre_grad_part, 0)
+        of_pre.pack()
+        of_pre.start()
+        reductions[0].start_b()
+
+        rows1 = 9 * shard_c
         r, _ = grid2(PART, 128)
+        sum_pre = mm(ones, pre_grad[...])
+        sum_mixed = mm(ones, mixed_grad[...])
         biases = jnp.where(
             r == 0,
             sum_pre,
             jnp.where(r == 1, sum_mixed[:, :128], jnp.where(r == 2, sum_mixed[:, 128:], 0.0)),
         ).astype(BF16)
         for s in range(n_space):
-            put(share0, s, rows2, biases)
-            left = n_snap * quarter - rows2 - PART
+            put(share1, s, rows1, biases)
+            left = n_snap * quarter - rows1 - PART
             if left:
-                put(share0, s, rows2 + PART, jnp.zeros((left, 128), BF16))
-        reductions[0].start_a()
-
-        rows1 = 9 * shard_c
+                put(share1, s, rows1 + PART, jnp.zeros((left, 128), BF16))
         all_sums = mm(pall[...], f3[...], TN)
         for b in range(3):
             sums = all_sums[:, b * channels : (b + 1) * channels]
@@ -515,13 +516,13 @@
                 t = 3 * a + b
                 for s in range(n_space):
                     put(share1, s, t * shard_c, part[s * shard_c : (s + 1) * shard_c])
-        for s in range(n_space):
-            left = n_snap * quarter - rows1
-            if left:
-                put(share1, s, rows1, jnp.zeros((left, 128), BF16))
         reductions[1].start_a()
-        reductions[0].start_b()
     else:
+        lax.fori_loop(0, CELLS // STEP, pre_grad_part, 0)
+        of_pre.pack()
+        of_pre.start()
+        sum_pre = mm(ones, pre_grad[...])
+        sum_mixed = mm(ones, mixed_grad[...])
         for b in range(3):
             sums = mm(hall[...], g3[:, pl.ds((2 - b) * channels, channels)], TN)
             for a in range(3):
@@ -532,12 +533,12 @@
         gb1[...] = sum_pre[0:1]
         gb2[...] = sum_mixed[0:1]
 
-    second.interior((h3, p3), hidden_channels)
-    second.wait_recv()
-    second.borders((h3, p3), hidden_channels)
-
+    of_hidden.interior(h3)
+    of_pre.interior(p3)
     if fused:
         reductions[1].start_b()
+    of_hidden.wait_recv()
+    of_hidden.borders(h3)
 
     def out_part(i, carry):
         here = rows_of(i, STEP)
@@ -565,6 +566,8 @@
     stores[0].start()
     if fused:
         reductions[0].start_c()
+    of_pre.wait_recv()
+    of_pre.borders(p3)
     lax.fori_loop(0, CELLS // STEP, grad_part, 0)
     stores[1].start()
     if fused:
@@ -586,7 +589,9 @@
         for t in range(9):
             for half in range(halves):
                 gw2[t, :, pl.ds(half * 128, 128)] = get((t * halves + half) * shard_h, shard_h)
-        tail = get(rows2, PART)
+        reductions[1].start_d()
+        reductions[1].finish(scale, whole)
+        tail = get(rows1, PART)
         r, c = grid2(128, shard_h)
         pick = jnp.where(r == c + me * shard_h, 1.0, 0.0)
         gb1[...] = jnp.dot(
@@ -602,28 +607,44 @@
                 0.0,
             )
         gb2[...] = jnp.sum(picked, axis=0, keepdims=True)
-
-        reductions[1].start_d()
-        reductions[1].finish(scale, whole)
         for t in range(9):
             gw1[t] = get(t * shard_c, shard_c)
         for red in reductions:
             red.wait_send()
-    first.wait_send()
-    second.wait_send()
+    for halo in halos:
+        halo.wait_send()
     for c in stores:
         c.wait()
 
 
-def store_all(*refs):
-    sem = refs[-1]
-    copies = [
-        pltpu.make_async_copy(refs[n], refs[6 + n], sem.at[n]) for n in range(6)
-    ]
-    for c in copies:
-        c.start()
-    for c in copies:
-        c.wait()
+def store_all(count, *refs):
+    ins, outs, held, in_sem, out_sem = (
+        refs[:count],
+        refs[count : 2 * count],
+        refs[2 * count : 3 * count],
+        refs[-2],
+        refs[-1],
+    )
+    pieces = []
+    for n in range(count):
+        rows = ins[n].shape[0]
+        parts = 4 if rows % 64 == 0 else 1
+        for k in range(parts):
+            where = pl.ds(k * (rows // parts), rows // parts)
+            i = len(pieces)
+            pieces.append(
+                (
+                    pltpu.make_async_copy(ins[n].at[where], held[n].at[where], in_sem.at[i]),
+                    pltpu.make_async_copy(held[n].at[where], outs[n].at[where], out_sem.at[i]),
+                )
+            )
+    for load, _ in pieces:
+        load.start()
+    for load, store in pieces:
+        load.wait()
+        store.start()
+    for _, store in pieces:
+        store.wait()
 
 
 def local(field_in, ocean_mask, cotangent, w_first, b_first, w_second, b_second):
@@ -642,15 +663,18 @@
             pltpu.VMEM((2, EDGE, width), BF16),
             pltpu.VMEM((4, BAND, width), BF16),
             pltpu.VMEM((4, PART, width), BF16),
-            pltpu.VMEM((cells + 2 * BAND, 3 * width // 2), BF16),
-            pltpu.VMEM((cells + 2 * BAND, 3 * width // 2), BF16),
             pltpu.SemaphoreType.DMA((8,)),
             pltpu.SemaphoreType.DMA((8,)),
         ]
 
-    scratch = halo_scratch(2 * channels) + halo_scratch(2 * hidden_channels)
+    widths = (channels, channels, hidden_channels, hidden_channels)
+    scratch = []
+    for width in widths:
+        scratch += halo_scratch(width)
+    scratch += [pltpu.VMEM((cells + 2 * BAND, 3 * width), BF16) for width in widths]
     scratch += [
         pltpu.VMEM((cells, 128), F32),
+        pltpu.VMEM((cells, hidden_channels), F32),
         pltpu.VMEM((cells + 2 * BAND, 3 * hidden_channels), BF16),
         pltpu.VMEM((cells + 2 * BAND, 3 * hidden_channels), BF16),
         pltpu.VMEM((3, 3 * hidden_channels, channels), BF16),
@@ -668,7 +692,7 @@
     ]
     if fused:
         chips = n_space // 2
-        need = max(9 * shard_c * hidden_channels // 128, 9 * shard_h * channels // 128 + PART)
+        need = max(9 * shard_c * hidden_channels // 128 + PART, 9 * shard_h * channels // 128)
         quarter = -(-need // (PART * n_snap)) * PART
         for _ in range(2):
             piece = (quarter, 128)
@@ -724,11 +748,13 @@
         b_second.reshape(1, channels),
     )
     field_out, grad_field, gw1, gw2, gb1, gb2 = pl.pallas_call(
-        store_all,
+        functools.partial(store_all, 6),
         out_shape=[jax.ShapeDtypeStruct(value.shape, value.dtype) for value in results],
         in_specs=[pl.BlockSpec(memory_space=pl.ANY)] * 6,
         out_specs=[pl.BlockSpec(memory_space=pl.ANY)] * 6,
-        scratch_shapes=[pltpu.SemaphoreType.DMA((6,))],
+        scratch_shapes=[pltpu.VMEM(value.shape, value.dtype) for value in results]
+        + [pltpu.SemaphoreType.DMA((12,)), pltpu.SemaphoreType.DMA((12,))],
+        compiler_params=pltpu.CompilerParams(vmem_limit_bytes=60 * 1024 * 1024),
     )(*results)
     whole_shape = field_in.shape
     if not fused:

time: 81.5 us -> 40.3 us (0.49)
  Pallas kernels: 80.6 us -> 39.5 us
    pallas_call x1, Pallas kernels: 41.9 us -> 2.26 us  [local(): pl.pallas_call(functools.partial(store_all, 6), out_shape=[jax.ShapeDtype...]
    pallas_call x1, Pallas kernels: 38.7 us -> 37.3 us  [local(): pl.pallas_call(functools.partial(kernel, n_space, n_snap, fused, scale),...]
where the time goes in v3:
time: 40.3 us; the launch traced here: 40.2 us
  Pallas kernels  39.5 us (98%)
  between operations  0.64 us (2%)
    pallas_call x1, Pallas kernels, local(): pl.pallas_call(functools.partial(kernel, n_space, n_snap, fused, scale),...  37.3 us
    pallas_call x1, Pallas kernels, local(): pl.pallas_call(functools.partial(store_all, 6), out_shape=[jax.ShapeDtype...  2.26 us

profile of v3, /device:TPU:0, one launch (start us, length us, event | category | flops | bytes accessed | tf_op | source)
XLA Modules:
  0.0 40.2 jit_solution(15890035048650767145)
XLA Ops:
  0.6 37.3 %shard_map.118 = (bf16[1024,256]{1,0:T(8,128)(2,1)}, bf16[1024,256]{1,0:T(8,128)(2,1)}, f32[9,32,128]{2,1,0:T(8,128)}, f32[9,16,256]{2,1,0:T(8,128)}, f32[1,16]{1,0:T(1,128)}, /*index=5*/f32[1,32]{1,0:T(1,128)}) custom-call(bf16[1024,256]{1,0:T(8,128)(2,1)} %bitcast.15, s32[32,32]{1,0:T(8,128)} %bitcast.17, bf16[1024,256]{1,0:T(8,128)(2,1)} %bitcast.16, ...), custom_call_target="tpu_custom_call" | custom-call | tf_op jit(solution)/shard_map/pallas_call | solution.py:732
  37.9 2.3 %shard_map.119 = (bf16[1024,256]{1,0:T(8,128)(2,1)}, bf16[1024,256]{1,0:T(8,128)(2,1)}, f32[9,32,128]{2,1,0:T(8,128)}, f32[9,16,256]{2,1,0:T(8,128)}, f32[1,16]{1,0:T(1,128)}, /*index=5*/f32[1,32]{1,0:T(1,128)}) custom-call(bf16[1024,256]{1,0:T(8,128)(2,1)} %get-tuple-element.18.refs_0_, bf16[1024,256]{1,0:T(8,128)(2,1)} %get-tuple-element.19.refs_1_, ...), custom_call_target="tpu_custom_call" | custom-call | tf_op jit(solution)/shard_map/pallas_call | solution.py:750

commit v4 on v3

--- a/solution.py
+++ b/solution.py
@@ -512,7 +512,7 @@
         for b in range(3):
             sums = all_sums[:, b * channels : (b + 1) * channels]
             for a in range(3):
-                part = sums[a * hidden_channels : (a + 1) * hidden_channels].T.astype(BF16)
+                part = sums[a * hidden_channels : (a + 1) * hidden_channels].astype(BF16).T
                 t = 3 * a + b
                 for s in range(n_space):
                     put(share1, s, t * shard_c, part[s * shard_c : (s + 1) * shard_c])

time: 40.3 us -> 40.3 us (level)
  no operation moved by 1% of the time
where the time goes in v4:
time: 40.3 us; the launch traced here: 40.2 us
  Pallas kernels  39.5 us (98%)
  between operations  0.64 us (2%)
    pallas_call x1, Pallas kernels, local(): pl.pallas_call(functools.partial(kernel, n_space, n_snap, fused, scale),...  37.3 us
    pallas_call x1, Pallas kernels, local(): pl.pallas_call(functools.partial(store_all, 6), out_shape=[jax.ShapeDtype...  2.26 us

profile of v4, /device:TPU:0, one launch (start us, length us, event | category | flops | bytes accessed | tf_op | source)
XLA Modules:
  0.0 40.2 jit_solution(12121456784795372640)
XLA Ops:
  0.6 37.3 %shard_map.118 = (bf16[1024,256]{1,0:T(8,128)(2,1)}, bf16[1024,256]{1,0:T(8,128)(2,1)}, f32[9,32,128]{2,1,0:T(8,128)}, f32[9,16,256]{2,1,0:T(8,128)}, f32[1,16]{1,0:T(1,128)}, /*index=5*/f32[1,32]{1,0:T(1,128)}) custom-call(bf16[1024,256]{1,0:T(8,128)(2,1)} %bitcast.15, s32[32,32]{1,0:T(8,128)} %bitcast.17, bf16[1024,256]{1,0:T(8,128)(2,1)} %bitcast.16, ...), custom_call_target="tpu_custom_call" | custom-call | tf_op jit(solution)/shard_map/pallas_call | solution.py:732
  37.9 2.3 %shard_map.119 = (bf16[1024,256]{1,0:T(8,128)(2,1)}, bf16[1024,256]{1,0:T(8,128)(2,1)}, f32[9,32,128]{2,1,0:T(8,128)}, f32[9,16,256]{2,1,0:T(8,128)}, f32[1,16]{1,0:T(1,128)}, /*index=5*/f32[1,32]{1,0:T(1,128)}) custom-call(bf16[1024,256]{1,0:T(8,128)(2,1)} %get-tuple-element.18.refs_0_, bf16[1024,256]{1,0:T(8,128)(2,1)} %get-tuple-element.19.refs_1_, ...), custom_call_target="tpu_custom_call" | custom-call | tf_op jit(solution)/shard_map/pallas_call | solution.py:750
